TPU v7x, 32 devices: a whole 2x2x4 slice. The times are simulated.
32 devices in a mesh: store: 8 (over y, x, core), tp: 4 (over z).
Axes of the slice: x: 2, y: 2, z: 4, core: 2. Of those that a mesh axis runs over, the one named last changes fastest.
Arguments:
- stored_hidden: bfloat16 [64, 128, 8192], P('store'), may hold values from -6 to 6
- kv_weight: bfloat16 [8192, 2, 1024], P(None, None, 'tp'), may hold values from -0.0625 to 0.0625
- new_query: bfloat16 [4096, 32, 128], P('store', 'tp'), may hold values from -176.7767 to 176.7767
- new_entries: bfloat16 [4096, 2, 8, 128], P('store', None, 'tp'), may hold values from -6.1 to 6.1
- out_weight: bfloat16 [4096, 4096], P('tp'), may hold values from -1.25 to 1.25
- prefix_len: int32 [16], replicated, may hold values from 257 to 512
- stretch_len: int32 [16], replicated, may hold values from 128 to 256
- block_loc: int32 [16, 4], replicated, may hold values from 0 to 63, as said below
- owner: int32 [16], replicated, may hold values from 0 to 15, as said below
Outputs:
- output: bfloat16 [4096, 4096], P('store', 'tp')
Inputs may be any that keep to these rules, and one draw needn't show every extreme that they name: `owner`: a permutation; serving slot g lies on store index g // 2. `block_loc`: every stored block is named once; the blocks of the requests served on one store index lie on distinct store indices, stored block b on store index b // 8; blocks from ceil(prefix_len / 128) on are not read.
All inputs are finite; a program needn't handle non-finite values.
Results may differ from a plain program's by a relative error of at most 0.012.
Values may be sent and summed in bfloat16 or wider, within the bound.
A program may use at most 192 MiB of HBM per device.

v0:
```python
import jax
import jax.numpy as jnp
from jax import lax
from jax.sharding import PartitionSpec as P

rope_base = 500000.0
mask_fill = -1e30


def rotary_at(values, positions):
    head = values.shape[-1]
    half = head // 2
    inverse = rope_base ** (-(jnp.arange(half, dtype=jnp.float32) * 2.0 / head))
    angles = positions.astype(jnp.float32)[..., None] * inverse
    cosine = jnp.cos(angles)[..., None, :]
    sine = jnp.sin(angles)[..., None, :]
    first = values[..., :half]
    second = values[..., half:]
    return jnp.concatenate(
        [first * cosine - second * sine, second * cosine + first * sine], axis=-1
    )


def shards(
    stored_hidden,
    kv_weight,
    new_query,
    new_entries,
    out_weight,
    prefix_len,
    stretch_len,
    block_loc,
    owner,
):
    stores = lax.axis_size("store")
    own_store = lax.axis_index("store")
    local_blocks, block_rows, width = stored_hidden.shape
    request_count = owner.shape[0]
    per_owner = request_count // stores
    span_count = block_loc.shape[1]
    span = span_count * block_rows
    head = new_query.shape[2]
    query_heads = new_query.shape[1]
    kv_local = kv_weight.shape[2] // head
    group = query_heads // kv_local
    stretch = new_query.shape[0] // per_owner
    slot_ids = jnp.arange(request_count, dtype=jnp.int32)
    matched = owner[None, :] == slot_ids[:, None]
    request_of = jnp.sum(jnp.where(matched, slot_ids[None, :], 0), axis=1)
    block_count = (prefix_len + block_rows - 1) // block_rows
    locations = block_loc.reshape(-1)
    holders = locations // local_blocks
    places = locations % local_blocks
    targets = jnp.broadcast_to((owner // per_owner)[:, None], block_loc.shape).reshape(-1)
    needed = (jnp.arange(span_count)[None, :] < block_count[:, None]).reshape(-1)
    chosen = (holders[None, :] == own_store) & (
        targets[None, :] == jnp.arange(stores, dtype=jnp.int32)[:, None]
    )
    picked = jnp.sum(jnp.where(chosen, places[None, :], 0), axis=1)
    present = jnp.any(chosen & needed[None, :], axis=1)
    my_slots = own_store * per_owner + jnp.arange(per_owner, dtype=jnp.int32)
    my_requests = request_of[my_slots]
    senders = (block_loc[my_requests] // local_blocks).reshape(-1)
    projection = kv_weight.reshape(width, -1)
    positions = jnp.arange(span, dtype=jnp.int32)[None, :]
    outgoing = jnp.where(
        present[:, None, None], stored_hidden[picked], jnp.zeros((), stored_hidden.dtype)
    )
    incoming = lax.all_to_all(outgoing, "store", split_axis=0, concat_axis=0, tiled=True)
    prefix_rows = incoming[senders].reshape(-1, width)
    projected = jnp.dot(prefix_rows, projection, preferred_element_type=jnp.float32)
    projected = projected.reshape(per_owner, span, 2, kv_local, head)
    keys = rotary_at(projected[:, :, 0], positions).astype(jnp.bfloat16)
    values = projected[:, :, 1].astype(jnp.bfloat16)
    queries = new_query.reshape(per_owner, stretch, kv_local, group, head)
    entries = new_entries.reshape(per_owner, stretch, 2, kv_local, head)
    scale = head ** (-0.5)
    early = (
        jnp.einsum("rqkgd,rpkd->rkgqp", queries, keys, preferred_element_type=jnp.float32) * scale
    )
    prefix_live = jnp.arange(span)[None, :] < prefix_len[my_requests][:, None]
    early = jnp.where(prefix_live[:, None, None, None, :], early, mask_fill)
    recent = (
        jnp.einsum(
            "rqkgd,rjkd->rkgqj", queries, entries[:, :, 0], preferred_element_type=jnp.float32
        )
        * scale
    )
    causal = jnp.arange(stretch)[None, :] <= jnp.arange(stretch)[:, None]
    recent = jnp.where(causal[None, None, None], recent, mask_fill)
    top = jnp.maximum(early.max(-1), recent.max(-1))[..., None]
    early_w = jnp.exp(early - top)
    recent_w = jnp.exp(recent - top)
    total = early_w.sum(-1, keepdims=True) + recent_w.sum(-1, keepdims=True)
    early_p = (early_w / total).astype(jnp.bfloat16)
    recent_p = (recent_w / total).astype(jnp.bfloat16)
    attended = jnp.einsum("rkgqp,rpkd->rqkgd", early_p, values, preferred_element_type=jnp.float32)
    attended = attended + jnp.einsum(
        "rkgqj,rjkd->rqkgd", recent_p, entries[:, :, 1], preferred_element_type=jnp.float32
    )
    attended = attended.astype(jnp.bfloat16).reshape(per_owner * stretch, query_heads * head)
    partial_value = (
        jnp.dot(attended, out_weight, preferred_element_type=jnp.float32)
        .astype(jnp.bfloat16)
        .astype(jnp.float32)
    )
    summed = lax.psum_scatter(
        partial_value.astype(jnp.bfloat16), "tp", scatter_dimension=1, tiled=True
    ).astype(jnp.float32)
    live = (jnp.arange(stretch)[None, :] < stretch_len[my_requests][:, None]).reshape(-1)
    return jnp.where(live[:, None], summed, 0.0).astype(jnp.bfloat16)


def solution(mesh):
    in_specs = (
        P("store", None, None),
        P(None, None, "tp"),
        P("store", "tp", None),
        P("store", None, "tp", None),
        P("tp", None),
        P(),
        P(),
        P(),
        P(),
    )
    out_specs = P("store", "tp")
    return jax.shard_map(shards, mesh=mesh, in_specs=in_specs, out_specs=out_specs, check_vma=False)
```

profile of v0, /device:TPU:10, one launch (start us, length us, event | category | flops | bytes accessed | tf_op | source)
XLA Modules:
  0.0 395.2 jit_solution(9046944318162300277)
XLA Ops:
  6.5 0.8 copy.32
  7.5 0.7 and_select_fusion.3
  8.5 11.7 %fusion.29 = (bf16[8,128,4096]{2,1,0:T(8,128)(2,1)}, bf16[8,128,4096]{2,1,0:T(8,128)(2,1)}) fusion(bf16[8,128,8192]{2,1,0:T(8,128)(2,1)} %param.9), kind=kLoop, calls=%fused_computation.92 | loop fusion | bytes 33554432 | tf_op jit(solution)/shard_map/gather | solution.py:67
  20.2 8.1 %gather_fusion.4 = bf16[8,128,4096]{2,1,0:T(8,128)(2,1)} fusion(bf16[8,128,4096]{2,1,0:T(8,128)(2,1)} %get-tuple-element.7, s32[1024]{0:T(1024)S(1)} %pad_clamp_fusion.1), kind=kCustom, calls=%fused_computation.4 | custom fusion | bytes 16777248 | tf_op jit(solution)/shard_map/gather | solution.py:67
  28.2 8.0 %gather_fusion.5 = bf16[8,128,4096]{2,1,0:T(8,128)(2,1)} fusion(bf16[8,128,4096]{2,1,0:T(8,128)(2,1)} %get-tuple-element.8, s32[1024]{0:T(1024)S(1)} %pad_clamp_fusion.1), kind=kCustom, calls=%fused_computation.5 | custom fusion | bytes 16777248 | tf_op jit(solution)/shard_map/gather | solution.py:67
  36.6 14.7 %maximum_select_fusion = bf16[8,128,8192]{2,1,0:T(8,128)(2,1)} fusion(bf16[8,128,4096]{2,1,0:T(8,128)(2,1)} %gather_fusion.5, bf16[8,128,4096]{2,1,0:T(8,128)(2,1)} %gather_fusion.4, pred[8]{0:T(512)(128)(4,1)S(1)} %fusion.17), kind=kLoop, calls=%fused_computation.8 | loop fusion | flops 41943040 | bytes 33554440 | tf_op jit(solution)/shard_map/jit(_where)/select_n | solution.py:66
  51.3 6.3 %all-to-all-start = ((bf16[8,128,8192]{2,1,0:T(8,128)(2,1)}), bf16[8,128,8192]{2,1,0:T(8,128)(2,1)}, u32[]{:S(2)}, u32[]{:S(2)}) async-start(bf16[8,128,8192]{2,1,0:T(8,128)(2,1)} %maximum_select_fusion), calls=%async_computation | async-start | bytes 33554432 | tf_op jit(solution)/shard_map/all_to_all | solution.py:69
  57.8 0.6 gather_fusion
  58.4 0.6 gather_fusion.2
  59.0 0.6 gather_fusion.3
  59.7 8.0 %copy.57 = bf16[1024,8,2,256]{3,1,2,0:T(8,128)(2,1)} copy(bf16[1024,8,2,256]{3,2,1,0:T(2,128)(2,1)} %bitcast.90) | data formatting | bytes 16777216
  67.7 11.4 %copy.34 = bf16[512,8192]{1,0:T(8,128)(2,1)} copy(bf16[512,8192]{0,1:T(8,128)(2,1)} %bitcast.88) | data formatting | bytes 16777216 | tf_op jit(solution)/shard_map/dot_general | solution.py:71
  79.3 0.5 multiply_cosine_fusion
  79.9 2.7 fusion.4
  82.6 157.6 %all-to-all-done = bf16[8,128,8192]{2,1,0:T(8,128)(2,1)} async-done(((bf16[8,128,8192]{2,1,0:T(8,128)(2,1)}), bf16[8,128,8192]{2,1,0:T(8,128)(2,1)}, u32[]{:S(2)}, u32[]{:S(2)}) %all-to-all-start) | async-done | bytes 16777248 | tf_op jit(solution)/shard_map/all_to_all | solution.py:69
  240.2 11.7 %fusion.28 = (bf16[8,128,4096]{2,1,0:T(8,128)(2,1)}, bf16[8,128,4096]{2,1,0:T(8,128)(2,1)}) fusion(bf16[8,128,8192]{2,1,0:T(8,128)(2,1)} %all-to-all-done), kind=kLoop, calls=%fused_computation.91 | loop fusion | bytes 33554432 | tf_op jit(solution)/shard_map/gather | solution.py:70
  251.9 8.1 %gather_fusion.6 = bf16[8,128,4096]{2,1,0:T(8,128)(2,1)} fusion(bf16[8,128,4096]{2,1,0:T(8,128)(2,1)} %get-tuple-element.5, s32[1024]{0:T(1024)S(1)} %pad_clamp_fusion), kind=kCustom, calls=%fused_computation.6 | custom fusion | bytes 16777248 | tf_op jit(solution)/shard_map/gather | solution.py:70
  259.9 8.0 %gather_fusion.7 = bf16[8,128,4096]{2,1,0:T(8,128)(2,1)} fusion(bf16[8,128,4096]{2,1,0:T(8,128)(2,1)} %get-tuple-element.6, s32[1024]{0:T(1024)S(1)} %pad_clamp_fusion), kind=kCustom, calls=%fused_computation.7 | custom fusion | bytes 16777248 | tf_op jit(solution)/shard_map/gather | solution.py:70
  268.0 8.0 %pad_maximum_fusion = bf16[8,128,8192]{2,1,0:T(8,128)(2,1)S(1)} fusion(bf16[8,128,4096]{2,1,0:T(8,128)(2,1)} %gather_fusion.7, bf16[8,128,4096]{2,1,0:T(8,128)(2,1)} %gather_fusion.6), kind=kLoop, calls=%fused_computation.9 | loop fusion | flops 33554432 | bytes 33554432
  276.0 12.3 %fusion.31 = f32[2,512,2,2,128]{1,4,3,2,0:T(8,128)S(1)} fusion(bf16[2,512,8192,1,1]{2,1,4,3,0:T(8,128)(2,1)S(1)} %bitcast.89, bf16[2,2,128,8192,1]{3,2,1,0,4:T(8,128)(2,1)} %bitcast.91), kind=kOutput, calls=%fused_computation.94 | convolution fusion | flops 8589934592 | bytes 27262976 | tf_op jit(solution)/shard_map/dot_general | solution.py:71
  288.4 0.2 subtract_convert_fusion
  288.6 2.2 bitcast_reduce_fusion
  290.8 0.9 fusion.3
  291.7 2.1 fusion.1
  293.8 1.2 fusion.6
  295.1 2.7 fusion.5
  297.7 0.8 copy.44
  298.5 0.8 reshape.349
  299.3 9.4 %convolution_convert_fusion = bf16[512,4096]{1,0:T(8,128)(2,1)} fusion(bf16[512,1024]{1,0:T(8,128)(2,1)S(1)} %reshape.349, bf16[1024,4096]{1,0:T(8,128)(2,1)} %param.13), kind=kOutput, calls=%fused_computation.16 | convolution fusion | flops 4297064448 | bytes 13631488 | tf_op jit(solution)/shard_map/dot_general | solution.py:103
  308.7 0.6 gather_fusion.1
  309.4 76.4 %reduce-scatter.2.cloned.1.call-done = bf16[512,1024]{1,0:T(8,128)(2,1)} async-done(((bf16[512,4096]{1,0:T(8,128)(2,1)}), bf16[512,1024]{1,0:T(8,128)(2,1)}) %reduce-scatter.2.cloned.1.call-update) | async-done | bytes 1048592 | tf_op jit(solution)/shard_map/reduce_scatter | solution.py:107
  385.9 2.4 select_convert_fusion
  (45 shorter events, 1.4 us)
Async XLA Ops:
  6.5 73.4 %copy-start = (bf16[512,8,128]{2,1,0:T(8,128)(2,1)S(1)}, bf16[512,8,128]{2,1,0:T(8,128)(2,1)}, u32[]{:S(2)}) copy-start(bf16[512,8,128]{2,1,0:T(8,128)(2,1)} %param.11) | copy-start | bytes 3145732
  28.2 8.0 %copy-start.1 = (s32[16]{0:T(128)S(1)}, s32[16]{0:T(128)}, u32[]{:S(2)}) copy-start(s32[16]{0:T(128)} %param.14) | copy-start | bytes 196
  51.3 6.3 %copy-start.5 = (s32[16]{0:T(128)S(1)}, s32[16]{0:T(128)}, u32[]{:S(2)}) copy-start(s32[16]{0:T(128)} %param.17) | copy-start | bytes 196
  51.3 188.9 %all-to-all-start = ((bf16[8,128,8192]{2,1,0:T(8,128)(2,1)}), bf16[8,128,8192]{2,1,0:T(8,128)(2,1)}, u32[]{:S(2)}, u32[]{:S(2)}) async-start(bf16[8,128,8192]{2,1,0:T(8,128)(2,1)} %maximum_select_fusion), calls=%async_computation | async-start | bytes 33554432 | tf_op jit(solution)/shard_map/all_to_all | solution.py:69
  57.6 328.3 %reduce-scatter.2.cloned.1.call-start = ((), (), s32[]{:S(2)}) async-start(), calls=%async_computation.2 | async-start | bytes 5242880 | tf_op jit(solution)/shard_map/reduce_scatter | solution.py:107
  67.7 11.4 %copy-start.4 = (bf16[512,2,2,128]{3,2,1,0:T(2,128)(2,1)S(1)}, bf16[512,2,2,128]{3,2,1,0:T(2,128)(2,1)}, u32[]{:S(2)}) copy-start(bf16[512,2,2,128]{3,2,1,0:T(2,128)(2,1)} %param.12) | copy-start | bytes 1572868
  288.3 2.5 copy-start.3
  299.3 9.4 %copy-start.2 = (s32[16]{0:T(128)S(1)}, s32[16]{0:T(128)}, u32[]{:S(2)}) copy-start(s32[16]{0:T(128)} %param.15) | copy-start | bytes 196
Sparse Core Ops, SparseCore 0:
  308.8 77.0 reduce-scatter.1
where the time goes:
time: 398 us; the launch traced here: 395 us
  waiting for transfers between devices  234 us (59%)
  local copies, waits for them, and re-layouts  80.4 us (20%)
  matrix products  30.5 us (8%)
  other arithmetic  30.3 us (8%)
  between operations  13.6 us (3%)
  starting transfers between devices  6.31 us (2%)
    all_to_all x1, waiting for transfers between devices, shards(): lax.all_to_all(outgoing, 'store', split_axis=0, concat_axis=0, tiled=True)  158 us
    reduce_scatter x1, waiting for transfers between devices, shards(): lax.psum_scatter(partial_value.astype(jnp.bfloat16), 'tp', scatter_dimens...  76.4 us
    gather x3, local copies, waits for them, and re-layouts, shards(): prefix_rows = incoming[senders].reshape(-1, width)  27.8 us
    gather x3, local copies, waits for them, and re-layouts, shards(): stored_hidden[picked]  27.8 us
    select_n x1, other arithmetic, shards(): jnp.where(present[:, None, None], stored_hidden[picked], jnp.zeros((), st...  14.7 us
    dot_general x1, matrix products, shards(): jnp.dot(prefix_rows, projection, preferred_element_type=jnp.float32)  12.3 us
    dot_general x1, local copies, waits for them, and re-layouts, shards(): jnp.dot(prefix_rows, projection, preferred_element_type=jnp.float32)  11.4 us
    dot_general x1, matrix products, shards(): jnp.dot(attended, out_weight, preferred_element_type=jnp.float32)  9.38 us
  transfers between devices with their start and end apart: 2, of which 2 were waited for; matrix products, arithmetic and copies ran while one was open for 6% of the time, Pallas kernels for 0%

commit v1 on v0

--- a/solution.py
+++ b/solution.py
@@ -47,31 +47,38 @@
     slot_ids = jnp.arange(request_count, dtype=jnp.int32)
     matched = owner[None, :] == slot_ids[:, None]
     request_of = jnp.sum(jnp.where(matched, slot_ids[None, :], 0), axis=1)
-    block_count = (prefix_len + block_rows - 1) // block_rows
     locations = block_loc.reshape(-1)
-    holders = locations // local_blocks
-    places = locations % local_blocks
-    targets = jnp.broadcast_to((owner // per_owner)[:, None], block_loc.shape).reshape(-1)
-    needed = (jnp.arange(span_count)[None, :] < block_count[:, None]).reshape(-1)
-    chosen = (holders[None, :] == own_store) & (
-        targets[None, :] == jnp.arange(stores, dtype=jnp.int32)[:, None]
-    )
-    picked = jnp.sum(jnp.where(chosen, places[None, :], 0), axis=1)
-    present = jnp.any(chosen & needed[None, :], axis=1)
     my_slots = own_store * per_owner + jnp.arange(per_owner, dtype=jnp.int32)
     my_requests = request_of[my_slots]
     senders = (block_loc[my_requests] // local_blocks).reshape(-1)
-    projection = kv_weight.reshape(width, -1)
-    positions = jnp.arange(span, dtype=jnp.int32)[None, :]
-    outgoing = jnp.where(
-        present[:, None, None], stored_hidden[picked], jnp.zeros((), stored_hidden.dtype)
+    local_ids = own_store * local_blocks + jnp.arange(local_blocks, dtype=jnp.int32)
+    entry_ids = jnp.arange(locations.shape[0], dtype=jnp.int32)
+    named = jnp.sum(
+        jnp.where(locations[None, :] == local_ids[:, None], entry_ids[None, :], 0), axis=1
     )
-    incoming = lax.all_to_all(outgoing, "store", split_axis=0, concat_axis=0, tiled=True)
-    prefix_rows = incoming[senders].reshape(-1, width)
-    projected = jnp.dot(prefix_rows, projection, preferred_element_type=jnp.float32)
-    projected = projected.reshape(per_owner, span, 2, kv_local, head)
-    keys = rotary_at(projected[:, :, 0], positions).astype(jnp.bfloat16)
-    values = projected[:, :, 1].astype(jnp.bfloat16)
+    target = owner[named // span_count] // per_owner
+    positions = (named % span_count)[:, None] * block_rows + jnp.arange(
+        block_rows, dtype=jnp.int32
+    )
+    hidden = stored_hidden.reshape(-1, width)
+    key_part = jnp.dot(hidden, kv_weight[:, 0], preferred_element_type=jnp.float32)
+    value_part = jnp.dot(hidden, kv_weight[:, 1], preferred_element_type=jnp.float32)
+    key_part = key_part.reshape(local_blocks, block_rows, kv_local, head)
+    key_part = rotary_at(key_part, positions).astype(jnp.bfloat16)
+    value_part = value_part.reshape(local_blocks, block_rows, kv_local, head).astype(jnp.bfloat16)
+    both = jnp.stack([key_part, value_part], axis=1)
+    slot = jnp.sum(
+        jnp.where(
+            target[None, :] == jnp.arange(stores, dtype=jnp.int32)[:, None],
+            jnp.arange(local_blocks, dtype=jnp.int32)[None, :],
+            0,
+        ),
+        axis=1,
+    )
+    incoming = lax.all_to_all(both[slot], "store", split_axis=0, concat_axis=0, tiled=True)
+    fetched = incoming[senders].reshape(per_owner, span_count, 2, block_rows, kv_local, head)
+    keys = fetched[:, :, 0].reshape(per_owner, span, kv_local, head)
+    values = fetched[:, :, 1].reshape(per_owner, span, kv_local, head)
     queries = new_query.reshape(per_owner, stretch, kv_local, group, head)
     entries = new_entries.reshape(per_owner, stretch, 2, kv_local, head)
     scale = head ** (-0.5)

time: 398 us -> 222 us (0.56)
  waiting for transfers between devices: 234 us -> 84.6 us
  other arithmetic: 30.3 us -> 7.28 us
  local copies, waits for them, and re-layouts: 80.4 us -> 67.6 us
  matrix products: 30.5 us -> 41.8 us
    all_to_all x1, waiting for transfers between devices: 158 us -> 8.77 us  [shards(): lax.all_to_all(both[slot], 'store', split_axis=0, concat_axis=0, tiled=True)]
    gather x6 -> x3, local copies, waits for them, and re-layouts: 55.6 us -> 3.05 us  [the longest x1 1.66 us: shards(): both[slot]]
    dot_general x1 -> x2, local copies, waits for them, and re-layouts: 11.4 us -> 34.6 us  [the longest x1 17.3 us: shards(): jnp.dot(hidden, kv_weight[:, 0], preferred_element_type=jnp.float32)]
    slice x0 -> x4, local copies, waits for them, and re-layouts: none -> 20.6 us  [the longest x1 18 us: shards(): kv_weight[:, 0]]
    select_n x6 -> x4, other arithmetic: 15.4 us -> 0.04 us  [the longest x2 0.02 us: shards(): target = owner[named // span_count] // per_owner]
    unnamed x1 -> x0, other arithmetic: 8.03 us -> none
    dot_general x1 -> x2, matrix products: 12.3 us -> 19.5 us  [the longest x1 9.96 us: shards(): jnp.dot(hidden, kv_weight[:, 0], preferred_element_type=jnp.float32)]
    unnamed x15 -> x20, local copies, waits for them, and re-layouts: 8.93 us -> 4.88 us
  transfers between devices with their start and end apart: 2 -> 2, of which waited for: 2 -> 2; matrix products, arithmetic and copies ran while one was open for 6% -> 3% of each run, Pallas kernels for 0% -> 0%
where the time goes in v1:
time: 222 us; the launch traced here: 219 us
  waiting for transfers between devices  84.6 us (38%)
  local copies, waits for them, and re-layouts  67.6 us (30%)
  matrix products  41.8 us (19%)
  between operations  13.7 us (6%)
  other arithmetic  7.28 us (3%)
  starting transfers between devices  4.25 us (2%)
    reduce_scatter x1, waiting for transfers between devices, shards(): lax.psum_scatter(partial_value.astype(jnp.bfloat16), 'tp', scatter_dimens...  75.8 us
    slice x1, local copies, waits for them, and re-layouts, shards(): kv_weight[:, 0]  18 us
    dot_general x1, local copies, waits for them, and re-layouts, shards(): jnp.dot(hidden, kv_weight[:, 0], preferred_element_type=jnp.float32)  17.3 us
    dot_general x1, local copies, waits for them, and re-layouts, shards(): jnp.dot(hidden, kv_weight[:, 1], preferred_element_type=jnp.float32)  17.3 us
    dot_general x1, matrix products, shards(): jnp.dot(hidden, kv_weight[:, 0], preferred_element_type=jnp.float32)  9.96 us
    dot_general x1, matrix products, shards(): jnp.dot(hidden, kv_weight[:, 1], preferred_element_type=jnp.float32)  9.57 us
    dot_general x1, matrix products, shards(): jnp.dot(attended, out_weight, preferred_element_type=jnp.float32)  9.47 us
    all_to_all x1, waiting for transfers between devices, shards(): lax.all_to_all(both[slot], 'store', split_axis=0, concat_axis=0, tiled=True)  8.77 us
  transfers between devices with their start and end apart: 2, of which 2 were waited for; matrix products, arithmetic and copies ran while one was open for 3% of the time, Pallas kernels for 0%

profile of v1, /device:TPU:10, one launch (start us, length us, event | category | flops | bytes accessed | tf_op | source)
XLA Modules:
  0.0 219.2 jit_solution(3460074218776221880)
XLA Ops:
  6.5 0.8 copy.42
  7.8 18.0 %fusion.35 = (bf16[8192,1,256]{2,1,0:T(2,128)(2,1)}, bf16[8192,1,256]{2,1,0:T(2,128)(2,1)}) fusion(bf16[8192,2,256]{2,1,0:T(2,128)(2,1)} %param.10), kind=kLoop, calls=%fused_computation.92 | loop fusion | bytes 16777216 | tf_op jit(solution)/shard_map/slice | solution.py:64
  25.8 17.3 %copy.71 = bf16[8192,1,256]{0,2,1:T(8,128)(2,1)} copy(bf16[8192,1,256]{2,1,0:T(2,128)(2,1)} %get-tuple-element.5) | data formatting | bytes 8388608 | tf_op jit(solution)/shard_map/dot_general | solution.py:64
  43.1 17.3 %copy.72 = bf16[8192,1,256]{0,2,1:T(8,128)(2,1)} copy(bf16[8192,1,256]{2,1,0:T(2,128)(2,1)} %get-tuple-element.6) | data formatting | bytes 8388608 | tf_op jit(solution)/shard_map/dot_general | solution.py:65
  60.4 10.0 %fusion.2 = f32[8,128,2,128]{1,3,2,0:T(8,128)S(1)} fusion(bf16[2,128,8192,1]{2,1,0,3:T(8,128)(2,1)} %bitcast.118, bf16[8,128,8192]{2,1,0:T(8,128)(2,1)} %param.9), kind=kOutput, calls=%fused_computation.9 | convolution fusion | flops 4294967296 | bytes 22020096 | tf_op jit(solution)/shard_map/dot_general | solution.py:64
  70.4 9.6 %fusion.14 = bf16[8,1,128,2,128]{2,4,3,0,1:T(8,128)(2,1)S(1)} fusion(bf16[2,128,8192,1]{2,1,0,3:T(8,128)(2,1)S(1)} %bitcast.119, bf16[8,128,8192]{2,1,0:T(8,128)(2,1)} %param.9), kind=kOutput, calls=%fused_computation.29 | convolution fusion | flops 4295229440 | bytes 21495808 | tf_op jit(solution)/shard_map/dot_general | solution.py:65
  80.0 0.6 gather_fusion.2
  80.8 1.0 multiply_cosine_fusion
  82.1 1.7 gather_fusion.3
  83.7 4.2 %all-to-all-start = ((bf16[8,2,128,2,128]{2,4,3,1,0:T(8,128)(2,1)}), bf16[8,2,128,2,128]{2,4,3,1,0:T(8,128)(2,1)S(1)}, u32[]{:S(2)}, u32[]{:S(2)}) async-start(bf16[8,2,128,2,128]{2,4,3,1,0:T(8,128)(2,1)} %gather_fusion.3), calls=%async_computation | async-start | bytes 2097152 | tf_op jit(solution)/shard_map/all_to_all | solution.py:78
  88.2 0.6 gather_fusion
  88.8 0.6 gather_fusion.4
  89.5 0.6 gather_fusion.6
  90.3 2.8 %fusion.8 = (f32[2,2,4,256]{3,2,1,0:T(4,128)S(1)}, f32[2,2,256,256,4]{3,2,4,1,0:T(8,128)}) fusion(pred[256,256]{0,1:T(8,128)(4,1)S(1)} %iota_compare_fusion, bf16[2,256,2,4,128]{4,3,2,1,0:T(4,128)(2,1)S(1)} %bitcast.117, bf16[2,256,1,2,128]{4,1,0,3,2:T(8,128)(2,1)S(1)} %get-tuple-element.12), kind=kOutput, calls=%fused_computation.23 | convolution fusion | flops 271577088 | bytes 5586944 | tf_op jit(solution)/shard_map/rqkgd,rjkd->rkgqj/dot_general | solution.py:91
  93.1 8.8 %all-to-all-done = bf16[8,2,128,2,128]{2,4,3,1,0:T(8,128)(2,1)S(1)} async-done(((bf16[8,2,128,2,128]{2,4,3,1,0:T(8,128)(2,1)}), bf16[8,2,128,2,128]{2,4,3,1,0:T(8,128)(2,1)S(1)}, u32[]{:S(2)}, u32[]{:S(2)}) %all-to-all-start) | async-done | bytes 1048608 | tf_op jit(solution)/shard_map/all_to_all | solution.py:78
  101.9 0.7 gather_fusion.5
  102.6 0.9 fusion.36
  103.5 1.3 copy.48
  104.8 1.6 bitcast_reduce_fusion
  106.5 1.9 fusion.5
  108.4 2.3 %copy-done.5 = f32[2,2,512,256,4]{3,2,4,1,0:T(8,128)} copy-done((f32[2,2,512,256,4]{3,2,4,1,0:T(8,128)}, f32[2,2,512,256,4]{3,2,4,1,0:T(8,128)S(1)}, u32[]{:S(2)}) %copy-start.5) | copy-done | bytes 8388632
  110.7 1.0 copy-done.6
  111.7 0.9 fusion.7
  113.2 3.4 %fusion.10 = f32[2,2,4,256,128]{3,4,2,1,0:T(8,128)S(1)} fusion(f32[2,2,256,256,4]{3,2,4,1,0:T(8,128)} %get-tuple-element.18, f32[2,2,4,256]{3,2,1,0:T(4,128)S(1)} %add.154, f32[2,2,4,256]{3,2,1,0:T(4,128)S(1)} %max.7, pred[256,256]{0,1:T(8,128)(4,1)S(1)} %iota_compare_fusion, bf16[2,256,1,2,128]{4,1,0,3,2:T(8,128)(2,1)S(1)} %get-tuple-element.11), kind=kOutput, calls=%fused_computation.27 | convolution fusion | flops 273678336 | bytes 6651904 | tf_op jit(solution)/shard_map/rkgqj,rjkd->rqkgd/dot_general | solution.py:105
  116.6 5.1 %fusion.9 = bf16[2,256,2,4,128]{1,4,3,2,0:T(8,128)(2,1)S(1)} fusion(f32[2,2,4,256,128]{3,4,2,1,0:T(8,128)S(1)} %fusion.10, f32[2,2,512,256,4]{3,2,4,1,0:T(8,128)} %copy-done.5, f32[2,2,4,256]{3,2,1,0:T(4,128)S(1)} %add.154, f32[2,2,4,256]{3,2,1,0:T(4,128)S(1)} %max.7, pred[2,512]{1,0:T(4,128)(4,1)S(1)} %iota_compare_fusion.2, ...), kind=kOutput, calls=%fused_computation.25 | convolution fusion | flops 548405248 | bytes 12092416 | tf_op jit(solution)/shard_map/rkgqp,rpkd->rqkgd/dot_general | solution.py:104
  121.7 0.8 copy.57
  122.5 0.8 reshape.359
  123.3 9.5 %convolution_convert_fusion = bf16[512,4096]{1,0:T(8,128)(2,1)} fusion(bf16[512,1024]{1,0:T(8,128)(2,1)S(1)} %reshape.359, bf16[1024,4096]{1,0:T(8,128)(2,1)} %param.13), kind=kOutput, calls=%fused_computation.17 | convolution fusion | flops 4297064448 | bytes 13631488 | tf_op jit(solution)/shard_map/dot_general | solution.py:110
  132.8 0.6 copy-done.4
  133.4 0.6 gather_fusion.1
  134.1 75.8 %reduce-scatter.2.cloned.1.call-done = bf16[512,1024]{1,0:T(8,128)(2,1)} async-done(((bf16[512,4096]{1,0:T(8,128)(2,1)}), bf16[512,1024]{1,0:T(8,128)(2,1)}) %reduce-scatter.2.cloned.1.call-update) | async-done | bytes 1048592 | tf_op jit(solution)/shard_map/reduce_scatter | solution.py:114
  209.9 2.4 %select_convert_fusion = bf16[512,1024]{1,0:T(8,128)(2,1)} fusion(bf16[512,1024]{1,0:T(8,128)(2,1)} %reduce-scatter.2.cloned.1.call-done, pred[512]{0:T(512)(128)(4,1)S(1)} %lt.100), kind=kLoop, calls=%fused_computation.26 | loop fusion | flops 1572864 | bytes 2097664 | tf_op jit(solution)/shard_map/convert_element_type | solution.py:118
  (49 shorter events, 2.0 us)
Async XLA Ops:
  6.5 83.8 %copy-start = (bf16[512,8,128]{2,1,0:T(8,128)(2,1)S(1)}, bf16[512,8,128]{2,1,0:T(8,128)(2,1)}, u32[]{:S(2)}) copy-start(bf16[512,8,128]{2,1,0:T(8,128)(2,1)} %param.11) | copy-start | bytes 3145732
  60.4 10.0 %copy-start.7 = (bf16[8192,1,256]{0,2,1:T(8,128)(2,1)S(1)}, bf16[8192,1,256]{0,2,1:T(8,128)(2,1)}, u32[]{:S(2)}) copy-start(bf16[8192,1,256]{0,2,1:T(8,128)(2,1)} %copy.72) | copy-start | bytes 12582916
  70.4 9.6 %copy-start.2 = (s32[16]{0:T(128)S(1)}, s32[16]{0:T(128)}, u32[]{:S(2)}) copy-start(s32[16]{0:T(128)} %param.17) | copy-start | bytes 196
  81.8 7.7 %copy-start.3 = (s32[16]{0:T(128)S(1)}, s32[16]{0:T(128)}, u32[]{:S(2)}) copy-start(s32[16]{0:T(128)} %param.14) | copy-start | bytes 196
  82.0 8.2 %copy-start.8 = (bf16[512,2,2,128]{3,2,1,0:T(2,128)(2,1)S(1)}, bf16[512,2,2,128]{3,2,1,0:T(2,128)(2,1)}, u32[]{:S(2)}) copy-start(bf16[512,2,2,128]{3,2,1,0:T(2,128)(2,1)} %param.12) | copy-start | bytes 1572868
  83.7 18.1 %all-to-all-start = ((bf16[8,2,128,2,128]{2,4,3,1,0:T(8,128)(2,1)}), bf16[8,2,128,2,128]{2,4,3,1,0:T(8,128)(2,1)S(1)}, u32[]{:S(2)}, u32[]{:S(2)}) async-start(bf16[8,2,128,2,128]{2,4,3,1,0:T(8,128)(2,1)} %gather_fusion.3), calls=%async_computation | async-start | bytes 2097152 | tf_op jit(solution)/shard_map/all_to_all | solution.py:78
  88.0 122.0 %reduce-scatter.2.cloned.1.call-start = ((), (), s32[]{:S(2)}) async-start(), calls=%async_computation.2 | async-start | bytes 5242880 | tf_op jit(solution)/shard_map/reduce_scatter | solution.py:114
  106.4 4.3 %copy-start.5 = (f32[2,2,512,256,4]{3,2,4,1,0:T(8,128)}, f32[2,2,512,256,4]{3,2,4,1,0:T(8,128)S(1)}, u32[]{:S(2)}) copy-start(f32[2,2,512,256,4]{3,2,4,1,0:T(8,128)S(1)} %get-tuple-element.16) | copy-start | bytes 25165828
  106.5 5.2 %copy-start.6 = (f32[2,2,256,256,4]{3,2,4,1,0:T(8,128)S(1)}, f32[2,2,256,256,4]{3,2,4,1,0:T(8,128)}, u32[]{:S(2)}) copy-start(f32[2,2,256,256,4]{3,2,4,1,0:T(8,128)} %get-tuple-element.18) | copy-start | bytes 12582916
  123.3 89.1 %copy-start.1 = (bf16[512,8,128]{2,1,0:T(8,128)(2,1)S(1)}, bf16[512,8,128]{2,1,0:T(8,128)(2,1)}, u32[]{:S(2)}) copy-start(bf16[512,8,128]{2,1,0:T(8,128)(2,1)} %param.11) | copy-start | bytes 3145732
  132.7 0.7 copy-start.4
Sparse Core Ops, SparseCore 0:
  132.9 77.0 reduce-scatter.1

commit v2 on v1

--- a/solution.py
+++ b/solution.py
@@ -1,6 +1,10 @@
+import functools
+
 import jax
 import jax.numpy as jnp
 from jax import lax
+from jax.experimental import pallas as pl
+from jax.experimental.pallas import tpu as pltpu
 from jax.sharding import PartitionSpec as P
 
 rope_base = 500000.0
@@ -19,6 +23,192 @@
     return jnp.concatenate(
         [first * cosine - second * sine, second * cosine + first * sine], axis=-1
     )
+
+
+def reduce_kernel(
+    groups,
+    pieces,
+    rows_ref,
+    weight_ref,
+    out_ref,
+    weight_buf,
+    part,
+    total,
+    from_left,
+    from_right,
+    weight_sem,
+    right_send,
+    right_recv,
+    left_send,
+    left_recv,
+):
+    me = lax.axis_index("tp")
+    wide = weight_buf.shape[3]
+    last = groups - 1
+    upper = jnp.where(me < groups // 2, 1, 0)
+
+    def group_at(step):
+        return upper * (last - step) + (1 - upper) * step
+
+    def weight_copy(group, piece):
+        start = pl.multiple_of((group * pieces + piece) * wide, wide)
+        return pltpu.make_async_copy(
+            weight_ref.at[:, pl.ds(start, wide)],
+            weight_buf.at[group, piece],
+            weight_sem.at[group, piece],
+        )
+
+    def right_copy(group, piece):
+        return pltpu.make_async_remote_copy(
+            src_ref=part.at[group, piece],
+            dst_ref=from_left.at[group, piece],
+            send_sem=right_send.at[group, piece],
+            recv_sem=right_recv.at[group, piece],
+            device_id={"tp": me + 1},
+            device_id_type=pl.DeviceIdType.MESH,
+        )
+
+    def left_copy(group, piece):
+        return pltpu.make_async_remote_copy(
+            src_ref=part.at[group, piece],
+            dst_ref=from_right.at[group, piece],
+            send_sem=left_send.at[group, piece],
+            recv_sem=left_recv.at[group, piece],
+            device_id={"tp": me - 1},
+            device_id_type=pl.DeviceIdType.MESH,
+        )
+
+    def each(body):
+        def step(index, carry):
+            body(index // pieces, index % pieces)
+            return carry
+
+        lax.fori_loop(0, groups * pieces, step, 0)
+
+    each(lambda step, piece: weight_copy(group_at(step), piece).start())
+
+    barrier = pltpu.get_barrier_semaphore()
+
+    @pl.when(me > 0)
+    def _():
+        pl.semaphore_signal(
+            barrier, inc=1, device_id={"tp": me - 1}, device_id_type=pl.DeviceIdType.MESH
+        )
+
+    @pl.when(me < last)
+    def _():
+        pl.semaphore_signal(
+            barrier, inc=1, device_id={"tp": me + 1}, device_id_type=pl.DeviceIdType.MESH
+        )
+
+    pl.semaphore_wait(barrier, jnp.where(me > 0, 1, 0) + jnp.where(me < last, 1, 0))
+
+    def produce(step, piece):
+        group = group_at(step)
+        weight_copy(group, piece).wait()
+        product = jnp.dot(
+            rows_ref[...], weight_buf[group, piece], preferred_element_type=jnp.float32
+        ).astype(part.dtype)
+        part[group, piece] = product
+
+        @pl.when(group == me)
+        def _():
+            total[piece] = product.astype(jnp.float32)
+
+        @pl.when((me == 0) & (group > me))
+        def _():
+            right_copy(group, piece).start()
+
+        @pl.when((me == last) & (group < me))
+        def _():
+            left_copy(group, piece).start()
+
+    each(produce)
+
+    def add(group, piece, arrived):
+        summed = part[group, piece].astype(jnp.float32) + arrived[group, piece].astype(jnp.float32)
+        part[group, piece] = summed.astype(part.dtype)
+
+    def pass_on(step, piece):
+        right = last - step
+
+        @pl.when((me > 0) & (right >= me))
+        def _():
+            right_copy(right, piece).wait_recv()
+
+        @pl.when((me > 0) & (right > me))
+        def _():
+            add(right, piece, from_left)
+            right_copy(right, piece).start()
+
+        @pl.when((me > 0) & (right == me))
+        def _():
+            total[piece] += from_left[right, piece].astype(jnp.float32)
+
+        left = step
+
+        @pl.when((me < last) & (left <= me))
+        def _():
+            left_copy(left, piece).wait_recv()
+
+        @pl.when((me < last) & (left < me))
+        def _():
+            add(left, piece, from_right)
+            left_copy(left, piece).start()
+
+        @pl.when((me < last) & (left == me))
+        def _():
+            total[piece] += from_right[left, piece].astype(jnp.float32)
+
+    each(pass_on)
+
+    for piece in range(pieces):
+        out_ref[:, piece * wide : (piece + 1) * wide] = total[piece].astype(out_ref.dtype)
+
+    def settle(group, piece):
+        @pl.when(group > me)
+        def _():
+            right_copy(group, piece).wait_send()
+
+        @pl.when(group < me)
+        def _():
+            left_copy(group, piece).wait_send()
+
+    each(settle)
+
+
+def projected_sum(rows, weight, groups):
+    count, depth = rows.shape
+    columns = weight.shape[1] // groups
+    pieces = 2
+    wide = columns // pieces
+    slots = (groups, pieces, count, wide)
+    return pl.pallas_call(
+        functools.partial(reduce_kernel, groups, pieces),
+        out_shape=jax.ShapeDtypeStruct((count, columns), jnp.bfloat16),
+        in_specs=[
+            pl.BlockSpec(memory_space=pltpu.VMEM),
+            pl.BlockSpec(memory_space=pl.ANY),
+        ],
+        out_specs=pl.BlockSpec(memory_space=pltpu.VMEM),
+        scratch_shapes=[
+            pltpu.VMEM((groups, pieces, depth, wide), jnp.bfloat16),
+            pltpu.VMEM(slots, jnp.bfloat16),
+            pltpu.VMEM((pieces, count, wide), jnp.float32),
+            pltpu.VMEM(slots, jnp.bfloat16),
+            pltpu.VMEM(slots, jnp.bfloat16),
+        ]
+        + [pltpu.SemaphoreType.DMA((groups, pieces))] * 5,
+        compiler_params=pltpu.CompilerParams(
+            collective_id=0, has_side_effects=True, vmem_limit_bytes=44 * 1024 * 1024
+        ),
+        cost_estimate=pl.CostEstimate(
+            flops=2 * count * depth * columns * groups,
+            bytes_accessed=weight.size * 2,
+            transcendentals=0,
+        ),
+        name="projected_sum",
+    )(rows, weight)
 
 
 def shards(
@@ -106,16 +296,9 @@
         "rkgqj,rjkd->rqkgd", recent_p, entries[:, :, 1], preferred_element_type=jnp.float32
     )
     attended = attended.astype(jnp.bfloat16).reshape(per_owner * stretch, query_heads * head)
-    partial_value = (
-        jnp.dot(attended, out_weight, preferred_element_type=jnp.float32)
-        .astype(jnp.bfloat16)
-        .astype(jnp.float32)
-    )
-    summed = lax.psum_scatter(
-        partial_value.astype(jnp.bfloat16), "tp", scatter_dimension=1, tiled=True
-    ).astype(jnp.float32)
     live = (jnp.arange(stretch)[None, :] < stretch_len[my_requests][:, None]).reshape(-1)
-    return jnp.where(live[:, None], summed, 0.0).astype(jnp.bfloat16)
+    attended = jnp.where(live[:, None], attended, jnp.zeros((), attended.dtype))
+    return projected_sum(attended, out_weight, lax.axis_size("tp"))
 
 
 def solution(mesh):

time: 222 us -> 213 us (0.959)
  Pallas kernels: 0 us -> 93.7 us
  waiting for transfers between devices: 84.6 us -> 8.04 us
  between operations: 13.7 us -> 0.33 us
  matrix products: 41.8 us -> 32.4 us
  other arithmetic: 7.28 us -> 4.98 us
    pallas_call x0 -> x1, Pallas kernels: none -> 93.7 us  [projected_sum(): pl.pallas_call(functools.partial(reduce_kernel, groups, pieces), out_shap...]
    reduce_scatter x1 -> x0, waiting for transfers between devices: 75.8 us -> none  [shards(): lax.psum_scatter(partial_value.astype(jnp.bfloat16), 'tp', scatter_dimens...]
    dot_general x1 -> x0, matrix products: 9.47 us -> none  [shards(): jnp.dot(attended, out_weight, preferred_element_type=jnp.float32)]
    convert_element_type x1 -> x0, other arithmetic: 2.44 us -> none  [shards(): return jnp.where(live[:, None], summed, 0.0).astype(jnp.bfloat16)]
    unnamed x20 -> x21, local copies, waits for them, and re-layouts: 4.88 us -> 5.23 us
  transfers between devices with their start and end apart: 2 -> 1, of which waited for: 2 -> 1; matrix products, arithmetic and copies ran while one was open for 3% -> 3% of each run, Pallas kernels for 0% -> 0%
where the time goes in v2:
time: 213 us; the launch traced here: 212 us
  Pallas kernels  93.7 us (44%)
  local copies, waits for them, and re-layouts  67.9 us (32%)
  matrix products  32.4 us (15%)
  waiting for transfers between devices  8.04 us (4%)
  other arithmetic  4.98 us (2%)
  starting transfers between devices  4.25 us (2%)
    pallas_call x1, Pallas kernels, projected_sum(): pl.pallas_call(functools.partial(reduce_kernel, groups, pieces), out_shap...  93.7 us
    slice x1, local copies, waits for them, and re-layouts, shards(): kv_weight[:, 0]  18 us
    dot_general x1, local copies, waits for them, and re-layouts, shards(): jnp.dot(hidden, kv_weight[:, 0], preferred_element_type=jnp.float32)  17.3 us
    dot_general x1, local copies, waits for them, and re-layouts, shards(): jnp.dot(hidden, kv_weight[:, 1], preferred_element_type=jnp.float32)  17.3 us
    dot_general x1, matrix products, shards(): jnp.dot(hidden, kv_weight[:, 0], preferred_element_type=jnp.float32)  9.96 us
    dot_general x1, matrix products, shards(): jnp.dot(hidden, kv_weight[:, 1], preferred_element_type=jnp.float32)  9.57 us
    all_to_all x1, waiting for transfers between devices, shards(): lax.all_to_all(both[slot], 'store', split_axis=0, concat_axis=0, tiled=True)  8.04 us
    unnamed x21, local copies, waits for them, and re-layouts  5.23 us
  transfers between devices with their start and end apart: 1, of which 1 were waited for; matrix products, arithmetic and copies ran while one was open for 3% of the time, Pallas kernels for 0%

profile of v2, /device:TPU:10, one launch (start us, length us, event | category | flops | bytes accessed | tf_op | source)
XLA Modules:
  0.0 211.6 jit_solution(2609033996786269672)
XLA Ops:
  0.0 0.8 copy.43
  1.2 18.0 %fusion.35 = (bf16[8192,1,256]{2,1,0:T(2,128)(2,1)}, bf16[8192,1,256]{2,1,0:T(2,128)(2,1)}) fusion(bf16[8192,2,256]{2,1,0:T(2,128)(2,1)} %param.10), kind=kLoop, calls=%fused_computation.91 | loop fusion | bytes 16777216 | tf_op jit(solution)/shard_map/slice | solution.py:254
  19.3 17.3 %copy.72 = bf16[8192,1,256]{0,2,1:T(8,128)(2,1)} copy(bf16[8192,1,256]{2,1,0:T(2,128)(2,1)} %get-tuple-element.5) | data formatting | bytes 8388608 | tf_op jit(solution)/shard_map/dot_general | solution.py:254
  36.6 17.3 %copy.73 = bf16[8192,1,256]{0,2,1:T(8,128)(2,1)} copy(bf16[8192,1,256]{2,1,0:T(2,128)(2,1)} %get-tuple-element.6) | data formatting | bytes 8388608 | tf_op jit(solution)/shard_map/dot_general | solution.py:255
  53.9 10.0 %fusion.2 = f32[8,128,2,128]{1,3,2,0:T(8,128)S(1)} fusion(bf16[2,128,8192,1]{2,1,0,3:T(8,128)(2,1)} %bitcast.116, bf16[8,128,8192]{2,1,0:T(8,128)(2,1)} %param.9), kind=kOutput, calls=%fused_computation.9 | convolution fusion | flops 4294967296 | bytes 22020096 | tf_op jit(solution)/shard_map/dot_general | solution.py:254
  63.9 9.6 %fusion.14 = bf16[8,1,128,2,128]{2,4,3,0,1:T(8,128)(2,1)S(1)} fusion(bf16[2,128,8192,1]{2,1,0,3:T(8,128)(2,1)S(1)} %bitcast.117, bf16[8,128,8192]{2,1,0:T(8,128)(2,1)} %param.9), kind=kOutput, calls=%fused_computation.27 | convolution fusion | flops 4295229440 | bytes 21495808 | tf_op jit(solution)/shard_map/dot_general | solution.py:255
  73.5 0.6 gather_fusion.2
  74.2 1.0 multiply_cosine_fusion
  75.6 1.7 gather_fusion.3
  77.2 4.2 %all-to-all-start = ((bf16[8,2,128,2,128]{2,4,3,1,0:T(8,128)(2,1)}), bf16[8,2,128,2,128]{2,4,3,1,0:T(8,128)(2,1)S(1)}, u32[]{:S(2)}, u32[]{:S(2)}) async-start(bf16[8,2,128,2,128]{2,4,3,1,0:T(8,128)(2,1)} %gather_fusion.3), calls=%async_computation | async-start | bytes 2097152 | tf_op jit(solution)/shard_map/all_to_all | solution.py:268
  81.6 0.6 gather_fusion
  82.3 0.6 gather_fusion.4
  83.0 0.6 gather_fusion.6
  83.7 0.6 gather_fusion.1
  84.5 2.8 %fusion.8 = (f32[2,2,4,256]{3,2,1,0:T(4,128)S(1)}, f32[2,2,256,256,4]{3,2,4,1,0:T(8,128)}) fusion(pred[256,256]{0,1:T(8,128)(4,1)S(1)} %iota_compare_fusion, bf16[2,256,2,4,128]{4,3,2,1,0:T(4,128)(2,1)S(1)} %bitcast.115, bf16[2,256,1,2,128]{4,1,0,3,2:T(8,128)(2,1)S(1)} %get-tuple-element.12), kind=kOutput, calls=%fused_computation.22 | convolution fusion | flops 271577088 | bytes 5586944 | tf_op jit(solution)/shard_map/rqkgd,rjkd->rkgqj/dot_general | solution.py:281
  87.3 8.0 %all-to-all-done = bf16[8,2,128,2,128]{2,4,3,1,0:T(8,128)(2,1)S(1)} async-done(((bf16[8,2,128,2,128]{2,4,3,1,0:T(8,128)(2,1)}), bf16[8,2,128,2,128]{2,4,3,1,0:T(8,128)(2,1)S(1)}, u32[]{:S(2)}, u32[]{:S(2)}) %all-to-all-start) | async-done | bytes 1048608 | tf_op jit(solution)/shard_map/all_to_all | solution.py:268
  95.4 0.7 gather_fusion.5
  96.1 0.9 fusion.36
  97.0 1.3 copy.49
  98.3 1.6 bitcast_reduce_fusion
  100.0 1.9 fusion.5
  101.9 2.3 %copy-done.5 = f32[2,2,512,256,4]{3,2,4,1,0:T(8,128)} copy-done((f32[2,2,512,256,4]{3,2,4,1,0:T(8,128)}, f32[2,2,512,256,4]{3,2,4,1,0:T(8,128)S(1)}, u32[]{:S(2)}) %copy-start.5) | copy-done | bytes 8388632
  104.2 1.0 copy-done.6
  105.2 0.9 fusion.7
  106.1 0.4 copy.48
  106.5 0.2 reshape.421
  106.7 3.4 %fusion.10 = f32[2,2,4,256,128]{3,4,2,1,0:T(8,128)S(1)} fusion(f32[2,2,256,256,4]{3,2,4,1,0:T(8,128)} %get-tuple-element.18, f32[2,2,4,256]{3,2,1,0:T(4,128)S(1)} %add.152, f32[2,2,4,256]{3,2,1,0:T(4,128)S(1)} %max.7, pred[256,256]{0,1:T(8,128)(4,1)S(1)} %iota_compare_fusion, bf16[2,256,1,2,128]{4,1,0,3,2:T(8,128)(2,1)S(1)} %get-tuple-element.11), kind=kOutput, calls=%fused_computation.25 | convolution fusion | flops 273678336 | bytes 6651904 | tf_op jit(solution)/shard_map/rkgqj,rjkd->rqkgd/dot_general | solution.py:295
  110.1 5.1 %fusion.9 = bf16[2,256,2,4,128]{1,4,3,2,0:T(8,128)(2,1)S(1)} fusion(f32[2,2,4,256,128]{3,4,2,1,0:T(8,128)S(1)} %fusion.10, f32[2,2,512,256,4]{3,2,4,1,0:T(8,128)} %copy-done.5, f32[2,2,4,256]{3,2,1,0:T(4,128)S(1)} %add.152, f32[2,2,4,256]{3,2,1,0:T(4,128)S(1)} %max.7, pred[2,512]{1,0:T(4,128)(4,1)S(1)} %iota_compare_fusion.2, ...), kind=kOutput, calls=%fused_computation.24 | convolution fusion | flops 548405248 | bytes 12092416 | tf_op jit(solution)/shard_map/rkgqp,rpkd->rqkgd/dot_general | solution.py:294
  115.2 0.8 copy.58
  116.0 0.8 reshape.359
  116.9 93.7 %projected_sum.1 = bf16[512,1024]{1,0:T(8,128)(2,1)S(1)} custom-call(bf16[512,1024]{1,0:T(8,128)(2,1)S(1)} %broadcast_select_fusion.rows_ref, bf16[1024,4096]{1,0:T(8,128)(2,1)} %weight_ref.1), custom_call_target="tpu_custom_call" | custom-call | flops 4294967296 | bytes 8388608 | tf_op jit(solution)/shard_map/projected_sum/pallas_call | solution.py:186
  210.6 1.0 copy.89
  (47 shorter events, 1.5 us)
Async XLA Ops:
  0.0 84.5 %copy-start = (bf16[512,8,128]{2,1,0:T(8,128)(2,1)S(1)}, bf16[512,8,128]{2,1,0:T(8,128)(2,1)}, u32[]{:S(2)}) copy-start(bf16[512,8,128]{2,1,0:T(8,128)(2,1)} %param.11) | copy-start | bytes 3145732
  53.9 10.0 %copy-start.7 = (bf16[8192,1,256]{0,2,1:T(8,128)(2,1)S(1)}, bf16[8192,1,256]{0,2,1:T(8,128)(2,1)}, u32[]{:S(2)}) copy-start(bf16[8192,1,256]{0,2,1:T(8,128)(2,1)} %copy.73) | copy-start | bytes 12582916
  63.8 9.6 %copy-start.2 = (s32[16]{0:T(128)S(1)}, s32[16]{0:T(128)}, u32[]{:S(2)}) copy-start(s32[16]{0:T(128)} %param.17) | copy-start | bytes 196
  75.2 7.7 %copy-start.3 = (s32[16]{0:T(128)S(1)}, s32[16]{0:T(128)}, u32[]{:S(2)}) copy-start(s32[16]{0:T(128)} %param.14) | copy-start | bytes 196
  75.4 8.2 %copy-start.8 = (bf16[512,2,2,128]{3,2,1,0:T(2,128)(2,1)S(1)}, bf16[512,2,2,128]{3,2,1,0:T(2,128)(2,1)}, u32[]{:S(2)}) copy-start(bf16[512,2,2,128]{3,2,1,0:T(2,128)(2,1)} %param.12) | copy-start | bytes 1572868
  75.4 8.2 %copy-start.4 = (s32[16]{0:T(128)S(1)}, s32[16]{0:T(128)}, u32[]{:S(2)}) copy-start(s32[16]{0:T(128)} %param.15) | copy-start | bytes 196
  77.2 18.1 %all-to-all-start = ((bf16[8,2,128,2,128]{2,4,3,1,0:T(8,128)(2,1)}), bf16[8,2,128,2,128]{2,4,3,1,0:T(8,128)(2,1)S(1)}, u32[]{:S(2)}, u32[]{:S(2)}) async-start(bf16[8,2,128,2,128]{2,4,3,1,0:T(8,128)(2,1)} %gather_fusion.3), calls=%async_computation | async-start | bytes 2097152 | tf_op jit(solution)/shard_map/all_to_all | solution.py:268
  99.9 4.3 %copy-start.5 = (f32[2,2,512,256,4]{3,2,4,1,0:T(8,128)}, f32[2,2,512,256,4]{3,2,4,1,0:T(8,128)S(1)}, u32[]{:S(2)}) copy-start(f32[2,2,512,256,4]{3,2,4,1,0:T(8,128)S(1)} %get-tuple-element.16) | copy-start | bytes 25165828
  100.0 5.2 %copy-start.6 = (f32[2,2,256,256,4]{3,2,4,1,0:T(8,128)S(1)}, f32[2,2,256,256,4]{3,2,4,1,0:T(8,128)}, u32[]{:S(2)}) copy-start(f32[2,2,256,256,4]{3,2,4,1,0:T(8,128)} %get-tuple-element.18) | copy-start | bytes 12582916
  116.9 94.7 %copy-start.1 = (bf16[512,8,128]{2,1,0:T(8,128)(2,1)S(1)}, bf16[512,8,128]{2,1,0:T(8,128)(2,1)}, u32[]{:S(2)}) copy-start(bf16[512,8,128]{2,1,0:T(8,128)(2,1)} %param.11) | copy-start | bytes 3145732

commit v3 on v2

--- a/solution.py
+++ b/solution.py
@@ -2,6 +2,7 @@
 
 import jax
 import jax.numpy as jnp
+import numpy as np
 from jax import lax
 from jax.experimental import pallas as pl
 from jax.experimental.pallas import tpu as pltpu
@@ -11,18 +12,162 @@
 mask_fill = -1e30
 
 
-def rotary_at(values, positions):
-    head = values.shape[-1]
+def rotary_table(span, head):
     half = head // 2
-    inverse = rope_base ** (-(jnp.arange(half, dtype=jnp.float32) * 2.0 / head))
-    angles = positions.astype(jnp.float32)[..., None] * inverse
-    cosine = jnp.cos(angles)[..., None, :]
-    sine = jnp.sin(angles)[..., None, :]
-    first = values[..., :half]
-    second = values[..., half:]
-    return jnp.concatenate(
-        [first * cosine - second * sine, second * cosine + first * sine], axis=-1
+    exponents = -(np.arange(half, dtype=np.float32) * np.float32(2.0 / head))
+    inverse = np.power(np.float32(rope_base), exponents)
+    angles = np.arange(span, dtype=np.float32)[:, None] * inverse[None, :]
+    cosine = np.cos(angles)
+    sine = np.sin(angles)
+    return (
+        np.concatenate([cosine, cosine], axis=1),
+        np.concatenate([-sine, sine], axis=1),
     )
+
+
+def project_kernel(
+    target_ref, place_ref, hidden_ref, weight_ref, cosine_ref, sine_ref, out_ref, key_sum, value_sum
+):
+    step = pl.program_id(0)
+    head = cosine_ref.shape[2]
+    wide = weight_ref.shape[2]
+    blocks, block_rows, depth = hidden_ref.shape
+    hidden = hidden_ref[...].reshape(blocks * block_rows, depth)
+    w = jnp.swapaxes(weight_ref[...],0,1)
+    key_part = jnp.dot(hidden, w[0], preferred_element_type=jnp.float32)
+    value_part = jnp.dot(hidden, w[1], preferred_element_type=jnp.float32)
+
+    @pl.when(step == 0)
+    def _():
+        key_sum[...] = key_part
+        value_sum[...] = value_part
+
+    @pl.when(step > 0)
+    def _():
+        key_sum[...] += key_part
+        value_sum[...] += value_part
+
+    @pl.when(step == pl.num_programs(0) - 1)
+    def _():
+        for block in range(blocks):
+            rows = pl.ds(block * block_rows, block_rows)
+            cosine = cosine_ref[place_ref[block]]
+            sine = sine_ref[place_ref[block]]
+            slot = target_ref[block]
+            for start in range(0, wide, head):
+                part = key_sum[rows, start : start + head]
+                turned = part * cosine + pltpu.roll(part, head // 2, 1) * sine
+                out_ref[slot, :, start : start + head] = turned.astype(out_ref.dtype)
+            out_ref[slot, :, wide:] = value_sum[rows, :].astype(out_ref.dtype)
+
+
+def project(target, place, hidden, weight, span_count, head, slots):
+    blocks, block_rows, width = hidden.shape
+    wide = weight.shape[2]
+    depth = 1024
+    cosine, sine = rotary_table(span_count * block_rows, head)
+    table = (span_count, block_rows, head)
+    whole = lambda shape: pl.BlockSpec(shape, lambda step, *_: (0,) * len(shape))
+    return pl.pallas_call(
+        project_kernel,
+        out_shape=jax.ShapeDtypeStruct((slots, block_rows, 2 * wide), jnp.bfloat16),
+        grid_spec=pltpu.PrefetchScalarGridSpec(
+            num_scalar_prefetch=2,
+            grid=(width // depth,),
+            in_specs=[
+                pl.BlockSpec((blocks, block_rows, depth), lambda step, *_: (0, 0, step)),
+                pl.BlockSpec((depth, 2, wide), lambda step, *_: (step, 0, 0)),
+                whole(table),
+                whole(table),
+            ],
+            out_specs=whole((slots, block_rows, 2 * wide)),
+            scratch_shapes=[pltpu.VMEM((blocks * block_rows, wide), jnp.float32)] * 2,
+        ),
+        compiler_params=pltpu.CompilerParams(vmem_limit_bytes=40 * 1024 * 1024),
+        name="project",
+    )(target, place, hidden, weight, cosine.reshape(table), sine.reshape(table))
+
+
+def attend_kernel(
+    sender_ref, prefix_ref, stretch_ref, query_ref, key_ref, value_ref, *block_refs_and_out
+):
+    block_refs, out_ref = block_refs_and_out[:-1], block_refs_and_out[-1]
+    request = pl.program_id(0)
+    heads, rows, head = query_ref.shape
+    kv_heads = key_ref.shape[0]
+    group = heads // kv_heads
+    span = len(block_refs) * block_refs[0].shape[1]
+    scale = head ** (-0.5)
+    prefix_live = lax.broadcasted_iota(jnp.int32, (rows, span), 1) < prefix_ref[request]
+    row_ids = lax.broadcasted_iota(jnp.int32, (rows, rows), 0)
+    causal = lax.broadcasted_iota(jnp.int32, (rows, rows), 1) <= row_ids
+    live = lax.broadcasted_iota(jnp.int32, (rows, head), 0) < stretch_ref[request]
+    contract_last = (((1,), (1,)), ((), ()))
+    for kv in range(kv_heads):
+        lanes = slice(kv * head, (kv + 1) * head)
+        value_lanes = slice((kv_heads + kv) * head, (kv_heads + kv + 1) * head)
+        keys = jnp.concatenate([ref[0, :, lanes] for ref in block_refs], axis=0)
+        values = jnp.concatenate([ref[0, :, value_lanes] for ref in block_refs], axis=0)
+        new_keys = key_ref[kv]
+        new_values = value_ref[kv]
+        for index in range(group):
+            h = kv * group + index
+            query = query_ref[h]
+            early = lax.dot_general(
+                query, keys, contract_last, preferred_element_type=jnp.float32
+            )
+            recent = lax.dot_general(
+                query, new_keys, contract_last, preferred_element_type=jnp.float32
+            )
+            early = jnp.where(prefix_live, early * scale, mask_fill)
+            recent = jnp.where(causal, recent * scale, mask_fill)
+            top = jnp.maximum(
+                jnp.max(early, axis=1, keepdims=True), jnp.max(recent, axis=1, keepdims=True)
+            )
+            early_w = jnp.exp(early - top)
+            recent_w = jnp.exp(recent - top)
+            total = jnp.sum(early_w, axis=1, keepdims=True) + jnp.sum(
+                recent_w, axis=1, keepdims=True
+            )
+            attended = jnp.dot(
+                early_w.astype(jnp.bfloat16), values, preferred_element_type=jnp.float32
+            ) + jnp.dot(
+                recent_w.astype(jnp.bfloat16), new_values, preferred_element_type=jnp.float32
+            )
+            attended = jnp.where(live, attended / total, 0.0)
+            out_ref[:, h * head : (h + 1) * head] = attended.astype(out_ref.dtype)
+
+
+def attend(senders, prefix_len, stretch_len, query, keys, values, incoming):
+    heads, count, head = query.shape
+    kv_heads = keys.shape[0]
+    requests = prefix_len.shape[0]
+    rows = count // requests
+    span_count = senders.shape[0] // requests
+    _, block_rows, wide = incoming.shape
+
+    def block_spec(j):
+        return pl.BlockSpec(
+            (1, block_rows, wide), lambda r, sender, *_: (sender[r * span_count + j], 0, 0)
+        )
+
+    return pl.pallas_call(
+        attend_kernel,
+        out_shape=jax.ShapeDtypeStruct((count, heads * head), jnp.bfloat16),
+        grid_spec=pltpu.PrefetchScalarGridSpec(
+            num_scalar_prefetch=3,
+            grid=(requests,),
+            in_specs=[
+                pl.BlockSpec((heads, rows, head), lambda r, *_: (0, r, 0)),
+                pl.BlockSpec((kv_heads, rows, head), lambda r, *_: (0, r, 0)),
+                pl.BlockSpec((kv_heads, rows, head), lambda r, *_: (0, r, 0)),
+            ]
+            + [block_spec(j) for j in range(span_count)],
+            out_specs=pl.BlockSpec((rows, heads * head), lambda r, *_: (r, 0)),
+        ),
+        compiler_params=pltpu.CompilerParams(vmem_limit_bytes=40 * 1024 * 1024),
+        name="attend",
+    )(senders, prefix_len, stretch_len, query, keys, values, *([incoming] * span_count))
 
 
 def reduce_kernel(
@@ -247,57 +392,19 @@
         jnp.where(locations[None, :] == local_ids[:, None], entry_ids[None, :], 0), axis=1
     )
     target = owner[named // span_count] // per_owner
-    positions = (named % span_count)[:, None] * block_rows + jnp.arange(
-        block_rows, dtype=jnp.int32
+    sent = project(
+        target, named % span_count, stored_hidden, kv_weight, span_count, head, stores
     )
-    hidden = stored_hidden.reshape(-1, width)
-    key_part = jnp.dot(hidden, kv_weight[:, 0], preferred_element_type=jnp.float32)
-    value_part = jnp.dot(hidden, kv_weight[:, 1], preferred_element_type=jnp.float32)
-    key_part = key_part.reshape(local_blocks, block_rows, kv_local, head)
-    key_part = rotary_at(key_part, positions).astype(jnp.bfloat16)
-    value_part = value_part.reshape(local_blocks, block_rows, kv_local, head).astype(jnp.bfloat16)
-    both = jnp.stack([key_part, value_part], axis=1)
-    slot = jnp.sum(
-        jnp.where(
-            target[None, :] == jnp.arange(stores, dtype=jnp.int32)[:, None],
-            jnp.arange(local_blocks, dtype=jnp.int32)[None, :],
-            0,
-        ),
-        axis=1,
+    incoming = lax.all_to_all(sent, "store", split_axis=0, concat_axis=0, tiled=True)
+    attended = attend(
+        senders,
+        prefix_len[my_requests],
+        stretch_len[my_requests],
+        jnp.transpose(new_query, (1, 0, 2)),
+        jnp.transpose(new_entries[:, 0], (1, 0, 2)),
+        jnp.transpose(new_entries[:, 1], (1, 0, 2)),
+        incoming,
     )
-    incoming = lax.all_to_all(both[slot], "store", split_axis=0, concat_axis=0, tiled=True)
-    fetched = incoming[senders].reshape(per_owner, span_count, 2, block_rows, kv_local, head)
-    keys = fetched[:, :, 0].reshape(per_owner, span, kv_local, head)
-    values = fetched[:, :, 1].reshape(per_owner, span, kv_local, head)
-    queries = new_query.reshape(per_owner, stretch, kv_local, group, head)
-    entries = new_entries.reshape(per_owner, stretch, 2, kv_local, head)
-    scale = head ** (-0.5)
-    early = (
-        jnp.einsum("rqkgd,rpkd->rkgqp", queries, keys, preferred_element_type=jnp.float32) * scale
-    )
-    prefix_live = jnp.arange(span)[None, :] < prefix_len[my_requests][:, None]
-    early = jnp.where(prefix_live[:, None, None, None, :], early, mask_fill)
-    recent = (
-        jnp.einsum(
-            "rqkgd,rjkd->rkgqj", queries, entries[:, :, 0], preferred_element_type=jnp.float32
-        )
-        * scale
-    )
-    causal = jnp.arange(stretch)[None, :] <= jnp.arange(stretch)[:, None]
-    recent = jnp.where(causal[None, None, None], recent, mask_fill)
-    top = jnp.maximum(early.max(-1), recent.max(-1))[..., None]
-    early_w = jnp.exp(early - top)
-    recent_w = jnp.exp(recent - top)
-    total = early_w.sum(-1, keepdims=True) + recent_w.sum(-1, keepdims=True)
-    early_p = (early_w / total).astype(jnp.bfloat16)
-    recent_p = (recent_w / total).astype(jnp.bfloat16)
-    attended = jnp.einsum("rkgqp,rpkd->rqkgd", early_p, values, preferred_element_type=jnp.float32)
-    attended = attended + jnp.einsum(
-        "rkgqj,rjkd->rqkgd", recent_p, entries[:, :, 1], preferred_element_type=jnp.float32
-    )
-    attended = attended.astype(jnp.bfloat16).reshape(per_owner * stretch, query_heads * head)
-    live = (jnp.arange(stretch)[None, :] < stretch_len[my_requests][:, None]).reshape(-1)
-    attended = jnp.where(live[:, None], attended, jnp.zeros((), attended.dtype))
     return projected_sum(attended, out_weight, lax.axis_size("tp"))
 
 

time: 213 us -> 145 us (0.68)
  local copies, waits for them, and re-layouts: 67.9 us -> 12.6 us
  matrix products: 32.4 us -> 0 us
  Pallas kernels: 93.7 us -> 118 us
  other arithmetic: 4.98 us -> 0.37 us
    dot_general x2 -> x0, local copies, waits for them, and re-layouts: 34.6 us -> none  [the longest x1 17.3 us: shards(): jnp.dot(hidden, kv_weight[:, 0], preferred_element_type=jnp.float32)]
    dot_general x6 -> x0, matrix products: 32.4 us -> none  [the longest x1 9.96 us: shards(): jnp.dot(hidden, kv_weight[:, 0], preferred_element_type=jnp.float32)]
    pallas_call x0 -> x2, Pallas kernels: none -> 24 us  [the longest x1 16.4 us: project(): pl.pallas_call(project_kernel, out_shape=jax.ShapeDtypeStruct((slots, blo...]
    slice x5 -> x1, local copies, waits for them, and re-layouts: 20.7 us -> 1.39 us  [shards(): new_entries[:, 1]]
    reduce_sum x3 -> x0, other arithmetic: 2.92 us -> none  [the longest x2 2.81 us: shards(): total = early_w.sum(-1, keepdims=True) + recent_w.sum(-1, keepdims=True)]
    gather x4 -> x2, local copies, waits for them, and re-layouts: 3.68 us -> 1.28 us  [the longest x1 0.64 us: shards(): prefix_len[my_requests]]
    unnamed x21 -> x17, local copies, waits for them, and re-layouts: 5.23 us -> 7.17 us
where the time goes in v3:
time: 145 us
  Pallas kernels  118 us (81%)
  local copies, waits for them, and re-layouts  12.6 us (9%)
  waiting for transfers between devices  9.54 us (7%)
  starting transfers between devices  4.26 us (3%)
    pallas_call x1, Pallas kernels, projected_sum(): pl.pallas_call(functools.partial(reduce_kernel, groups, pieces), out_shap...  93.8 us
    pallas_call x1, Pallas kernels, project(): pl.pallas_call(project_kernel, out_shape=jax.ShapeDtypeStruct((slots, blo...  16.4 us
    all_to_all x1, waiting for transfers between devices, shards(): lax.all_to_all(sent, 'store', split_axis=0, concat_axis=0, tiled=True)  9.54 us
    pallas_call x1, Pallas kernels, attend(): pl.pallas_call(attend_kernel, out_shape=jax.ShapeDtypeStruct((count, head...  7.59 us
    unnamed x17, local copies, waits for them, and re-layouts  7.17 us
    all_to_all x1, starting transfers between devices, shards(): lax.all_to_all(sent, 'store', split_axis=0, concat_axis=0, tiled=True)  4.26 us
  transfers between devices with their start and end apart: 1, of which 1 were waited for; matrix products, arithmetic and copies ran while one was open for 3% of the time, Pallas kernels for 0%

profile of v3, /device:TPU:10, one launch (start us, length us, event | category | flops | bytes accessed | tf_op | source)
XLA Modules:
  0.0 144.6 jit_solution(578149279909774523)
XLA Ops:
  0.0 0.0 copy-start
  0.0 0.8 copy.22
  0.8 0.1 eq.33
  0.9 0.2 select_reduce_fusion.1
  1.1 1.3 gather_fusion.4
  2.4 0.0 copy-start.1
  2.4 3.4 %copy-done.1 = bf16[8192,2,256]{2,1,0:T(2,128)(2,1)S(1)} copy-done((bf16[8192,2,256]{2,1,0:T(2,128)(2,1)S(1)}, bf16[8192,2,256]{2,1,0:T(2,128)(2,1)}, u32[]{:S(2)}) %copy-start.1) | copy-done | bytes 8388632
  5.8 0.0 copy-start.2
  5.8 0.9 copy-done.2
  6.7 0.0 copy-start.3
  6.7 0.9 copy-done.3
  7.7 0.0 copy-start.4
  7.7 0.0 copy-start.5
  7.7 16.4 %project.1 = bf16[8,128,512]{2,1,0:T(8,128)(2,1)} custom-call(s32[8]{0:T(128)S(1)} %get-tuple-element.10.target_ref, s32[8]{0:T(128)S(1)} %get-tuple-element.9.place_ref, bf16[8,128,8192]{2,1,0:T(8,128)(2,1)} %hidden_ref.1, bf16[8192,2,256]{2,1,0:T(2,128)(2,1)S(1)} %copy-done.1, f32[4,128,128]{2,1,0:T(8,128)S(1)} %copy-done.3, f32[4,128,128]{2,1,0:T(8,128)S(1)} %copy-done.2), custom_call_target="tpu_custom_call" | custom-call | tf_op jit(solution)/shard_map/project/pallas_call | solution.py:71
  24.1 4.3 %all-to-all-start = ((bf16[8,128,512]{2,1,0:T(8,128)(2,1)}), bf16[8,128,512]{2,1,0:T(8,128)(2,1)S(1)}, u32[]{:S(2)}, u32[]{:S(2)}) async-start(bf16[8,128,512]{2,1,0:T(8,128)(2,1)} %project.1), calls=%async_computation | async-start | bytes 2097152 | tf_op jit(solution)/shard_map/all_to_all | solution.py:398
  28.4 0.0 copy-done.4
  28.4 0.1 select_reduce_fusion
  28.5 0.6 gather_fusion
  29.2 0.6 gather_fusion.1
  29.7 0.0 copy-done
  29.7 0.6 gather_fusion.3
  30.4 0.0 copy-done.5
  30.4 0.6 gather_fusion.2
  31.0 0.1 gather.22
  31.1 0.0 copy-done.6
  31.1 0.1 copy.32
  31.2 1.4 fusion.4
  32.6 0.1 copy_bitcast_fusion.1
  32.7 9.5 %all-to-all-done.block_refs_and_out_0_.block_refs_and_out_1_.block_refs_and_out_2_.block_refs_and_out_3_ = bf16[8,128,512]{2,1,0:T(8,128)(2,1)S(1)} async-done(((bf16[8,128,512]{2,1,0:T(8,128)(2,1)}), bf16[8,128,512]{2,1,0:T(8,128)(2,1)S(1)}, u32[]{:S(2)}, u32[]{:S(2)}) %all-to-all-start) | async-done | bytes 1048608 | tf_op jit(solution)/shard_map/all_to_all | solution.py:398
  42.3 7.6 %attend.1.rows_ref = bf16[512,1024]{1,0:T(8,128)(2,1)S(1)} custom-call(s32[8]{0:T(128)S(1)} %and_select_fusion.3.sender_ref, s32[2]{0:T(128)S(1)} %gather_fusion.2, s32[2]{0:T(128)S(1)} %gather_fusion.3, bf16[8,512,128]{2,1,0:T(8,128)(2,1)S(1)} %bitcast.29, bf16[2,512,128]{2,1,0:T(8,128)(2,1)S(1)} %get-tuple-element.8.key_ref, ...), custom_call_target="tpu_custom_call" | custom-call | tf_op jit(solution)/shard_map/attend/pallas_call | solution.py:154
  49.9 93.8 %projected_sum.1 = bf16[512,1024]{1,0:T(8,128)(2,1)S(1)} custom-call(bf16[512,1024]{1,0:T(8,128)(2,1)S(1)} %attend.1.rows_ref, bf16[1024,4096]{1,0:T(8,128)(2,1)} %weight_ref.3), custom_call_target="tpu_custom_call" | custom-call | flops 4294967296 | bytes 8388608 | tf_op jit(solution)/shard_map/projected_sum/pallas_call | solution.py:331
  143.6 1.0 copy.34
  (10 shorter events, 0.1 us)
Async XLA Ops:
  0.0 29.7 %copy-start = (s32[16]{0:T(128)S(1)}, s32[16]{0:T(128)}, u32[]{:S(2)}) copy-start(s32[16]{0:T(128)} %param.17) | copy-start | bytes 196
  2.4 3.4 %copy-start.1 = (bf16[8192,2,256]{2,1,0:T(2,128)(2,1)S(1)}, bf16[8192,2,256]{2,1,0:T(2,128)(2,1)}, u32[]{:S(2)}) copy-start(bf16[8192,2,256]{2,1,0:T(2,128)(2,1)} %weight_ref.2) | copy-start | bytes 25165828
  5.8 0.9 copy-start.2
  6.7 0.9 copy-start.3
  7.7 20.7 %copy-start.4 = (s32[16]{0:T(128)S(1)}, s32[16]{0:T(128)}, u32[]{:S(2)}) copy-start(s32[16]{0:T(128)} %param.19) | copy-start | bytes 196
  7.7 22.7 %copy-start.5 = (s32[16]{0:T(128)S(1)}, s32[16]{0:T(128)}, u32[]{:S(2)}) copy-start(s32[16]{0:T(128)} %param.16) | copy-start | bytes 196
  7.7 23.4 %copy-start.6 = (bf16[512,8,128]{2,1,0:T(8,128)(2,1)S(1)}, bf16[512,8,128]{2,1,0:T(8,128)(2,1)}, u32[]{:S(2)}) copy-start(bf16[512,8,128]{2,1,0:T(8,128)(2,1)} %param.13) | copy-start | bytes 3145732
  24.1 18.2 %all-to-all-start = ((bf16[8,128,512]{2,1,0:T(8,128)(2,1)}), bf16[8,128,512]{2,1,0:T(8,128)(2,1)S(1)}, u32[]{:S(2)}, u32[]{:S(2)}) async-start(bf16[8,128,512]{2,1,0:T(8,128)(2,1)} %project.1), calls=%async_computation | async-start | bytes 2097152 | tf_op jit(solution)/shard_map/all_to_all | solution.py:398

commit v4 on v3

--- a/solution.py
+++ b/solution.py
@@ -83,7 +83,7 @@
             out_specs=whole((slots, block_rows, 2 * wide)),
             scratch_shapes=[pltpu.VMEM((blocks * block_rows, wide), jnp.float32)] * 2,
         ),
-        compiler_params=pltpu.CompilerParams(vmem_limit_bytes=40 * 1024 * 1024),
+        compiler_params=pltpu.CompilerParams(vmem_limit_bytes=60 * 1024 * 1024),
         name="project",
     )(target, place, hidden, weight, cosine.reshape(table), sine.reshape(table))
 
@@ -274,38 +274,59 @@
         summed = part[group, piece].astype(jnp.float32) + arrived[group, piece].astype(jnp.float32)
         part[group, piece] = summed.astype(part.dtype)
 
-    def pass_on(step, piece):
-        right = last - step
-
-        @pl.when((me > 0) & (right >= me))
-        def _():
-            right_copy(right, piece).wait_recv()
-
-        @pl.when((me > 0) & (right > me))
-        def _():
-            add(right, piece, from_left)
-            right_copy(right, piece).start()
-
-        @pl.when((me > 0) & (right == me))
-        def _():
-            total[piece] += from_left[right, piece].astype(jnp.float32)
-
-        left = step
-
-        @pl.when((me < last) & (left <= me))
-        def _():
-            left_copy(left, piece).wait_recv()
-
-        @pl.when((me < last) & (left < me))
-        def _():
-            add(left, piece, from_right)
-            left_copy(left, piece).start()
-
-        @pl.when((me < last) & (left == me))
-        def _():
-            total[piece] += from_right[left, piece].astype(jnp.float32)
-
-    each(pass_on)
+    def pass_right(index):
+        group, piece = last - index // pieces, index % pieces
+
+        @pl.when(group >= me)
+        def _():
+            right_copy(group, piece).wait_recv()
+
+        @pl.when(group > me)
+        def _():
+            add(group, piece, from_left)
+            right_copy(group, piece).start()
+
+        @pl.when(group == me)
+        def _():
+            total[piece] += from_left[group, piece].astype(jnp.float32)
+
+    def pass_left(index):
+        group, piece = index // pieces, index % pieces
+
+        @pl.when(group <= me)
+        def _():
+            left_copy(group, piece).wait_recv()
+
+        @pl.when(group < me)
+        def _():
+            add(group, piece, from_right)
+            left_copy(group, piece).start()
+
+        @pl.when(group == me)
+        def _():
+            total[piece] += from_right[group, piece].astype(jnp.float32)
+
+    count = groups * pieces
+
+    def pass_on(index, carry):
+        right = index - (1 - upper)
+        left = index - upper
+
+        @pl.when((upper == 1) & (me > 0) & (right < count))
+        def _():
+            pass_right(right)
+
+        @pl.when((me < last) & (left >= 0) & (left < count))
+        def _():
+            pass_left(left)
+
+        @pl.when((upper == 0) & (me > 0) & (right >= 0))
+        def _():
+            pass_right(right)
+
+        return carry
+
+    lax.fori_loop(0, count + 1, pass_on, 0)
 
     for piece in range(pieces):
         out_ref[:, piece * wide : (piece + 1) * wide] = total[piece].astype(out_ref.dtype)
@@ -325,7 +346,7 @@
 def projected_sum(rows, weight, groups):
     count, depth = rows.shape
     columns = weight.shape[1] // groups
-    pieces = 2
+    pieces = 4
     wide = columns // pieces
     slots = (groups, pieces, count, wide)
     return pl.pallas_call(
@@ -391,7 +412,8 @@
     named = jnp.sum(
         jnp.where(locations[None, :] == local_ids[:, None], entry_ids[None, :], 0), axis=1
     )
-    target = owner[named // span_count] // per_owner
+    naming = (named // span_count)[:, None] == slot_ids[None, :]
+    target = jnp.sum(jnp.where(naming, owner[None, :], 0), axis=1) // per_owner
     sent = project(
         target, named % span_count, stored_hidden, kv_weight, span_count, head, stores
     )

time: 145 us -> 121 us (0.83)
  Pallas kernels: 118 us -> 97.7 us
  local copies, waits for them, and re-layouts: 12.6 us -> 6 us
  other arithmetic: 0.37 us -> 2.24 us
    pallas_call x1, Pallas kernels: 93.8 us -> 72.3 us  [projected_sum(): pl.pallas_call(functools.partial(reduce_kernel, groups, pieces), out_shap...]
    unnamed x17 -> x11, local copies, waits for them, and re-layouts: 7.17 us -> 1.89 us
  transfers between devices with their start and end apart: 1 -> 1, of which waited for: 1 -> 1; matrix products, arithmetic and copies ran while one was open for 3% -> 4% of each run, Pallas kernels for 0% -> 0%
where the time goes in v4:
time: 121 us; the launch traced here: 120 us
  Pallas kernels  97.7 us (81%)
  waiting for transfers between devices  9.54 us (8%)
  local copies, waits for them, and re-layouts  6 us (5%)
  starting transfers between devices  4.26 us (4%)
  other arithmetic  2.24 us (2%)
    pallas_call x1, Pallas kernels, projected_sum(): pl.pallas_call(functools.partial(reduce_kernel, groups, pieces), out_shap...  72.3 us
    pallas_call x1, Pallas kernels, project(): pl.pallas_call(project_kernel, out_shape=jax.ShapeDtypeStruct((slots, blo...  17.8 us
    all_to_all x1, waiting for transfers between devices, shards(): lax.all_to_all(sent, 'store', split_axis=0, concat_axis=0, tiled=True)  9.54 us
    pallas_call x1, Pallas kernels, attend(): pl.pallas_call(attend_kernel, out_shape=jax.ShapeDtypeStruct((count, head...  7.59 us
    all_to_all x1, starting transfers between devices, shards(): lax.all_to_all(sent, 'store', split_axis=0, concat_axis=0, tiled=True)  4.26 us
  transfers between devices with their start and end apart: 1, of which 1 were waited for; matrix products, arithmetic and copies ran while one was open for 4% of the time, Pallas kernels for 0%

profile of v4, /device:TPU:10, one launch (start us, length us, event | category | flops | bytes accessed | tf_op | source)
XLA Modules:
  0.0 119.8 jit_solution(11234420667638745538)
XLA Ops:
  0.0 0.0 copy-start
  0.0 0.8 copy.22
  0.8 0.1 eq.46
  0.9 0.2 select_reduce_fusion.2
  1.0 0.5 and_select_fusion
  1.6 0.8 select_reduce_fusion.1
  2.4 0.5 and_select_fusion.1.target_ref
  3.0 0.0 copy-start.3
  3.0 0.0 copy-start.1
  3.0 0.0 copy-start.2
  3.0 17.8 %project.1 = bf16[8,128,512]{2,1,0:T(8,128)(2,1)} custom-call(s32[8]{0:T(128)} %and_select_fusion.1.target_ref, s32[8]{0:T(128)} %get-tuple-element.7.place_ref, bf16[8,128,8192]{2,1,0:T(8,128)(2,1)} %hidden_ref.1, bf16[8192,2,256]{2,1,0:T(2,128)(2,1)} %weight_ref.2, f32[4,128,128]{2,1,0:T(8,128)} %constant.64.clone.cosine_ref, ...), custom_call_target="tpu_custom_call" | custom-call | tf_op jit(solution)/shard_map/project/pallas_call | solution.py:71
  20.8 4.3 %all-to-all-start = ((bf16[8,128,512]{2,1,0:T(8,128)(2,1)}), bf16[8,128,512]{2,1,0:T(8,128)(2,1)S(1)}, u32[]{:S(2)}, u32[]{:S(2)}) async-start(bf16[8,128,512]{2,1,0:T(8,128)(2,1)} %project.1), calls=%async_computation | async-start | bytes 2097152 | tf_op jit(solution)/shard_map/all_to_all | solution.py:420
  25.0 0.0 copy-done.3
  25.0 0.1 select_reduce_fusion
  25.2 0.6 gather_fusion
  25.8 0.6 gather_fusion.1
  26.4 0.0 copy-done
  26.4 0.6 gather_fusion.3
  27.0 0.0 copy-done.1
  27.0 0.6 gather_fusion.2
  27.7 0.1 gather.19
  27.8 0.0 copy-done.2
  27.8 0.1 copy.32
  27.9 1.4 %fusion.2 = (bf16[512,1,2,128]{3,2,1,0:T(2,128)(2,1)S(1)}, bf16[512,1,2,128]{3,2,1,0:T(2,128)(2,1)S(1)}) fusion(bf16[512,2,2,128]{3,2,1,0:T(2,128)(2,1)} %param.14), kind=kLoop, calls=%fused_computation.32 | loop fusion | bytes 1048576 | tf_op jit(solution)/shard_map/slice | solution.py:427
  29.3 0.1 copy_bitcast_fusion.1
  29.4 9.5 %all-to-all-done.block_refs_and_out_0_.block_refs_and_out_1_.block_refs_and_out_2_.block_refs_and_out_3_ = bf16[8,128,512]{2,1,0:T(8,128)(2,1)S(1)} async-done(((bf16[8,128,512]{2,1,0:T(8,128)(2,1)}), bf16[8,128,512]{2,1,0:T(8,128)(2,1)S(1)}, u32[]{:S(2)}, u32[]{:S(2)}) %all-to-all-start) | async-done | bytes 1048608 | tf_op jit(solution)/shard_map/all_to_all | solution.py:420
  38.9 7.6 %attend.1.rows_ref = bf16[512,1024]{1,0:T(8,128)(2,1)S(1)} custom-call(s32[8]{0:T(128)S(1)} %and_select_fusion.3.sender_ref, s32[2]{0:T(128)S(1)} %gather_fusion.2, s32[2]{0:T(128)S(1)} %gather_fusion.3, bf16[8,512,128]{2,1,0:T(8,128)(2,1)S(1)} %bitcast.17, bf16[2,512,128]{2,1,0:T(8,128)(2,1)S(1)} %get-tuple-element.10.key_ref, ...), custom_call_target="tpu_custom_call" | custom-call | tf_op jit(solution)/shard_map/attend/pallas_call | solution.py:154
  46.5 72.3 %projected_sum.1 = bf16[512,1024]{1,0:T(8,128)(2,1)S(1)} custom-call(bf16[512,1024]{1,0:T(8,128)(2,1)S(1)} %attend.1.rows_ref, bf16[1024,4096]{1,0:T(8,128)(2,1)} %weight_ref.3), custom_call_target="tpu_custom_call" | custom-call | flops 4294967296 | bytes 8388608 | tf_op jit(solution)/shard_map/projected_sum/pallas_call | solution.py:352
  118.8 1.0 copy.34
  (6 shorter events, 0.0 us)
Async XLA Ops:
  0.0 26.4 %copy-start = (s32[16]{0:T(128)S(1)}, s32[16]{0:T(128)}, u32[]{:S(2)}) copy-start(s32[16]{0:T(128)} %param.17) | copy-start | bytes 196
  3.0 22.1 %copy-start.3 = (s32[16]{0:T(128)S(1)}, s32[16]{0:T(128)}, u32[]{:S(2)}) copy-start(s32[16]{0:T(128)} %param.19) | copy-start | bytes 196
  3.0 24.1 %copy-start.1 = (s32[16]{0:T(128)S(1)}, s32[16]{0:T(128)}, u32[]{:S(2)}) copy-start(s32[16]{0:T(128)} %param.16) | copy-start | bytes 196
  3.0 24.8 %copy-start.2 = (bf16[512,8,128]{2,1,0:T(8,128)(2,1)S(1)}, bf16[512,8,128]{2,1,0:T(8,128)(2,1)}, u32[]{:S(2)}) copy-start(bf16[512,8,128]{2,1,0:T(8,128)(2,1)} %param.13) | copy-start | bytes 3145732
  20.8 18.2 %all-to-all-start = ((bf16[8,128,512]{2,1,0:T(8,128)(2,1)}), bf16[8,128,512]{2,1,0:T(8,128)(2,1)S(1)}, u32[]{:S(2)}, u32[]{:S(2)}) async-start(bf16[8,128,512]{2,1,0:T(8,128)(2,1)} %project.1), calls=%async_computation | async-start | bytes 2097152 | tf_op jit(solution)/shard_map/all_to_all | solution.py:420

commit v5 on v4

--- a/solution.py
+++ b/solution.py
@@ -26,26 +26,21 @@
 
 
 def project_kernel(
-    target_ref, place_ref, hidden_ref, weight_ref, cosine_ref, sine_ref, out_ref, key_sum, value_sum
+    target_ref, place_ref, hidden_ref, weight_ref, cosine_ref, sine_ref, out_ref, sums
 ):
     step = pl.program_id(0)
     head = cosine_ref.shape[2]
     wide = weight_ref.shape[2]
     blocks, block_rows, depth = hidden_ref.shape
     hidden = hidden_ref[...].reshape(blocks * block_rows, depth)
-    w = jnp.swapaxes(weight_ref[...],0,1)
-    key_part = jnp.dot(hidden, w[0], preferred_element_type=jnp.float32)
-    value_part = jnp.dot(hidden, w[1], preferred_element_type=jnp.float32)
+    parts = jnp.swapaxes(weight_ref[...], 0, 1)
+    both = jnp.concatenate([parts[0], parts[1]], axis=1)
 
     @pl.when(step == 0)
     def _():
-        key_sum[...] = key_part
-        value_sum[...] = value_part
-
-    @pl.when(step > 0)
-    def _():
-        key_sum[...] += key_part
-        value_sum[...] += value_part
+        sums[...] = jnp.zeros_like(sums)
+
+    sums[...] += jnp.dot(hidden, both, preferred_element_type=jnp.float32)
 
     @pl.when(step == pl.num_programs(0) - 1)
     def _():
@@ -55,16 +50,16 @@
             sine = sine_ref[place_ref[block]]
             slot = target_ref[block]
             for start in range(0, wide, head):
-                part = key_sum[rows, start : start + head]
+                part = sums[rows, start : start + head]
                 turned = part * cosine + pltpu.roll(part, head // 2, 1) * sine
                 out_ref[slot, :, start : start + head] = turned.astype(out_ref.dtype)
-            out_ref[slot, :, wide:] = value_sum[rows, :].astype(out_ref.dtype)
-
-
-def project(target, place, hidden, weight, span_count, head, slots):
+            out_ref[slot, :, wide:] = sums[rows, wide:].astype(out_ref.dtype)
+
+
+def project(target, place, hidden, weight, span_count, head, slots, kv):
     blocks, block_rows, width = hidden.shape
-    wide = weight.shape[2]
-    depth = 1024
+    wide = head
+    depth = 2048
     cosine, sine = rotary_table(span_count * block_rows, head)
     table = (span_count, block_rows, head)
     whole = lambda shape: pl.BlockSpec(shape, lambda step, *_: (0,) * len(shape))
@@ -76,14 +71,17 @@
             grid=(width // depth,),
             in_specs=[
                 pl.BlockSpec((blocks, block_rows, depth), lambda step, *_: (0, 0, step)),
-                pl.BlockSpec((depth, 2, wide), lambda step, *_: (step, 0, 0)),
+                pl.BlockSpec((depth, 2, wide), lambda step, *_: (step, 0, kv)),
                 whole(table),
                 whole(table),
             ],
             out_specs=whole((slots, block_rows, 2 * wide)),
-            scratch_shapes=[pltpu.VMEM((blocks * block_rows, wide), jnp.float32)] * 2,
+            scratch_shapes=[pltpu.VMEM((blocks * block_rows, 2 * wide), jnp.float32)],
         ),
         compiler_params=pltpu.CompilerParams(vmem_limit_bytes=60 * 1024 * 1024),
+        cost_estimate=pl.CostEstimate(
+            flops=4 * hidden.size * wide, bytes_accessed=2 * hidden.size, transcendentals=0
+        ),
         name="project",
     )(target, place, hidden, weight, cosine.reshape(table), sine.reshape(table))
 
@@ -96,7 +94,8 @@
     heads, rows, head = query_ref.shape
     kv_heads = key_ref.shape[0]
     group = heads // kv_heads
-    span = len(block_refs) * block_refs[0].shape[1]
+    span_count = len(block_refs) // kv_heads
+    span = span_count * block_refs[0].shape[1]
     scale = head ** (-0.5)
     prefix_live = lax.broadcasted_iota(jnp.int32, (rows, span), 1) < prefix_ref[request]
     row_ids = lax.broadcasted_iota(jnp.int32, (rows, rows), 0)
@@ -104,10 +103,9 @@
     live = lax.broadcasted_iota(jnp.int32, (rows, head), 0) < stretch_ref[request]
     contract_last = (((1,), (1,)), ((), ()))
     for kv in range(kv_heads):
-        lanes = slice(kv * head, (kv + 1) * head)
-        value_lanes = slice((kv_heads + kv) * head, (kv_heads + kv + 1) * head)
-        keys = jnp.concatenate([ref[0, :, lanes] for ref in block_refs], axis=0)
-        values = jnp.concatenate([ref[0, :, value_lanes] for ref in block_refs], axis=0)
+        own_refs = block_refs[kv * span_count : (kv + 1) * span_count]
+        keys = jnp.concatenate([ref[0, :, :head] for ref in own_refs], axis=0)
+        values = jnp.concatenate([ref[0, :, head:] for ref in own_refs], axis=0)
         new_keys = key_ref[kv]
         new_values = value_ref[kv]
         for index in range(group):
@@ -144,7 +142,7 @@
     requests = prefix_len.shape[0]
     rows = count // requests
     span_count = senders.shape[0] // requests
-    _, block_rows, wide = incoming.shape
+    _, block_rows, wide = incoming[0].shape
 
     def block_spec(j):
         return pl.BlockSpec(
@@ -162,12 +160,12 @@
                 pl.BlockSpec((kv_heads, rows, head), lambda r, *_: (0, r, 0)),
                 pl.BlockSpec((kv_heads, rows, head), lambda r, *_: (0, r, 0)),
             ]
-            + [block_spec(j) for j in range(span_count)],
+            + [block_spec(j) for j in range(span_count)] * kv_heads,
             out_specs=pl.BlockSpec((rows, heads * head), lambda r, *_: (r, 0)),
         ),
         compiler_params=pltpu.CompilerParams(vmem_limit_bytes=40 * 1024 * 1024),
         name="attend",
-    )(senders, prefix_len, stretch_len, query, keys, values, *([incoming] * span_count))
+    )(senders, prefix_len, stretch_len, query, keys, values, *[blocks for blocks in incoming for _ in range(span_count)])
 
 
 def reduce_kernel(
@@ -414,10 +412,12 @@
     )
     naming = (named // span_count)[:, None] == slot_ids[None, :]
     target = jnp.sum(jnp.where(naming, owner[None, :], 0), axis=1) // per_owner
-    sent = project(
-        target, named % span_count, stored_hidden, kv_weight, span_count, head, stores
-    )
-    incoming = lax.all_to_all(sent, "store", split_axis=0, concat_axis=0, tiled=True)
+    incoming = []
+    for kv in range(kv_local):
+        sent = project(
+            target, named % span_count, stored_hidden, kv_weight, span_count, head, stores, kv
+        )
+        incoming.append(lax.all_to_all(sent, "store", split_axis=0, concat_axis=0, tiled=True))
     attended = attend(
         senders,
         prefix_len[my_requests],

time: 121 us -> 129 us (1.066)
  Pallas kernels: 97.7 us -> 104 us
  starting transfers between devices: 4.26 us -> 8.45 us
  waiting for transfers between devices: 9.54 us -> 8.2 us
    pallas_call x1 -> x2, Pallas kernels: 17.8 us -> 24.1 us  [project(): pl.pallas_call(project_kernel, out_shape=jax.ShapeDtypeStruct((slots, blo...]
    all_to_all x1 -> x2, starting transfers between devices: 4.26 us -> 8.45 us  [shards(): lax.all_to_all(sent, 'store', split_axis=0, concat_axis=0, tiled=True)]
    all_to_all x1 -> x2, waiting for transfers between devices: 9.54 us -> 8.2 us  [shards(): lax.all_to_all(sent, 'store', split_axis=0, concat_axis=0, tiled=True)]
  transfers between devices with their start and end apart: 1 -> 2, of which waited for: 1 -> 1; matrix products, arithmetic and copies ran while one was open for 4% -> 3% of each run, Pallas kernels for 0% -> 9%
where the time goes in v5:
time: 129 us; the launch traced here: 128 us
  Pallas kernels  104 us (81%)
  starting transfers between devices  8.45 us (7%)
  waiting for transfers between devices  8.2 us (6%)
  local copies, waits for them, and re-layouts  4.97 us (4%)
  other arithmetic  2.28 us (2%)
    pallas_call x1, Pallas kernels, projected_sum(): pl.pallas_call(functools.partial(reduce_kernel, groups, pieces), out_shap...  72.3 us
    pallas_call x2, Pallas kernels, project(): pl.pallas_call(project_kernel, out_shape=jax.ShapeDtypeStruct((slots, blo...  24.1 us
    all_to_all x2, starting transfers between devices, shards(): lax.all_to_all(sent, 'store', split_axis=0, concat_axis=0, tiled=True)  8.45 us
    all_to_all x2, waiting for transfers between devices, shards(): lax.all_to_all(sent, 'store', split_axis=0, concat_axis=0, tiled=True)  8.2 us
    pallas_call x1, Pallas kernels, attend(): pl.pallas_call(attend_kernel, out_shape=jax.ShapeDtypeStruct((count, head...  7.53 us
  transfers between devices with their start and end apart: 2, of which 1 were waited for; matrix products, arithmetic and copies ran while one was open for 3% of the time, Pallas kernels for 9%

profile of v5, /device:TPU:10, one launch (start us, length us, event | category | flops | bytes accessed | tf_op | source)
XLA Modules:
  0.0 127.9 jit_solution(6989507111652783976)
XLA Ops:
  0.0 0.0 copy-start
  0.0 0.8 copy.24
  0.8 0.1 eq.47
  0.9 0.2 select_reduce_fusion.2
  1.0 0.5 and_select_fusion
  1.6 0.8 select_reduce_fusion.1
  2.4 0.6 and_select_fusion.1.target_ref
  3.0 0.0 copy-start.4
  3.0 0.0 copy-start.3
  3.0 12.1 %project.3 = bf16[8,128,256]{2,1,0:T(8,128)(2,1)} custom-call(s32[8]{0:T(128)} %and_select_fusion.1.target_ref, s32[8]{0:T(128)} %get-tuple-element.7.place_ref, bf16[8,128,8192]{2,1,0:T(8,128)(2,1)} %hidden_ref.3, bf16[8192,2,256]{2,1,0:T(2,128)(2,1)} %weight_ref.4, f32[4,128,128]{2,1,0:T(8,128)} %constant.67.clone.cosine_ref, ...), custom_call_target="tpu_custom_call" | custom-call | flops 4294967296 | bytes 16777216 | tf_op jit(solution)/shard_map/project/pallas_call | solution.py:66
  15.1 4.3 %all-to-all-start.1 = ((bf16[8,128,256]{2,1,0:T(8,128)(2,1)}), bf16[8,128,256]{2,1,0:T(8,128)(2,1)S(1)}, u32[]{:S(2)}, u32[]{:S(2)}) async-start(bf16[8,128,256]{2,1,0:T(8,128)(2,1)} %project.3), calls=%async_computation.1 | async-start | bytes 1048576 | tf_op jit(solution)/shard_map/all_to_all | solution.py:420
  19.4 0.0 copy-done.4
  19.4 0.1 select_reduce_fusion
  19.5 0.6 gather_fusion
  20.2 0.0 copy-done.3
  20.2 0.4 fusion.2
  20.6 0.6 gather_fusion.1
  21.1 0.0 copy-done
  21.1 0.6 gather_fusion.3
  21.8 0.0 copy-done.1
  21.8 0.6 gather_fusion.2
  22.4 0.1 gather.19
  22.5 0.0 copy-done.2
  22.5 0.1 copy.34
  22.6 12.0 %project.2 = bf16[8,128,256]{2,1,0:T(8,128)(2,1)} custom-call(s32[8]{0:T(128)} %and_select_fusion.1.target_ref, s32[8]{0:T(128)} %get-tuple-element.7.place_ref, bf16[8,128,8192]{2,1,0:T(8,128)(2,1)} %hidden_ref.3, bf16[8192,2,256]{2,1,0:T(2,128)(2,1)} %weight_ref.4, f32[4,128,128]{2,1,0:T(8,128)} %constant.67.clone.cosine_ref, ...), custom_call_target="tpu_custom_call" | custom-call | flops 4294967296 | bytes 16777216 | tf_op jit(solution)/shard_map/project/pallas_call | solution.py:66
  34.6 0.0 all-to-all-done.1.block_refs_and_out_4_.block_refs_and_out_5_.block_refs_and_out_6_.block_refs_and_out_7_
  34.6 4.2 %all-to-all-start = ((bf16[8,128,256]{2,1,0:T(8,128)(2,1)}), bf16[8,128,256]{2,1,0:T(8,128)(2,1)S(1)}, u32[]{:S(2)}, u32[]{:S(2)}) async-start(bf16[8,128,256]{2,1,0:T(8,128)(2,1)} %project.2), calls=%async_computation | async-start | bytes 1048576 | tf_op jit(solution)/shard_map/all_to_all | solution.py:420
  38.8 0.1 copy_bitcast_fusion.1
  38.9 8.2 %all-to-all-done.block_refs_and_out_0_.block_refs_and_out_1_.block_refs_and_out_2_.block_refs_and_out_3_ = bf16[8,128,256]{2,1,0:T(8,128)(2,1)S(1)} async-done(((bf16[8,128,256]{2,1,0:T(8,128)(2,1)}), bf16[8,128,256]{2,1,0:T(8,128)(2,1)S(1)}, u32[]{:S(2)}, u32[]{:S(2)}) %all-to-all-start) | async-done | bytes 524320 | tf_op jit(solution)/shard_map/all_to_all | solution.py:420
  47.1 7.5 %attend.1.rows_ref = bf16[512,1024]{1,0:T(8,128)(2,1)S(1)} custom-call(s32[8]{0:T(128)S(1)} %and_select_fusion.3.sender_ref, s32[2]{0:T(128)S(1)} %gather_fusion.2, s32[2]{0:T(128)S(1)} %gather_fusion.3, bf16[8,512,128]{2,1,0:T(8,128)(2,1)S(1)} %bitcast.17, bf16[2,512,128]{2,1,0:T(8,128)(2,1)S(1)} %get-tuple-element.10.key_ref, ...), custom_call_target="tpu_custom_call" | custom-call | tf_op jit(solution)/shard_map/attend/pallas_call | solution.py:152
  54.7 72.3 %projected_sum.1 = bf16[512,1024]{1,0:T(8,128)(2,1)S(1)} custom-call(bf16[512,1024]{1,0:T(8,128)(2,1)S(1)} %attend.1.rows_ref, bf16[1024,4096]{1,0:T(8,128)(2,1)} %weight_ref.5), custom_call_target="tpu_custom_call" | custom-call | flops 4294967296 | bytes 8388608 | tf_op jit(solution)/shard_map/projected_sum/pallas_call | solution.py:350
  126.9 1.0 copy.36
  (8 shorter events, 0.0 us)
Async XLA Ops:
  0.0 21.1 %copy-start = (s32[16]{0:T(128)S(1)}, s32[16]{0:T(128)}, u32[]{:S(2)}) copy-start(s32[16]{0:T(128)} %param.19) | copy-start | bytes 196
  3.0 16.4 %copy-start.4 = (s32[16]{0:T(128)S(1)}, s32[16]{0:T(128)}, u32[]{:S(2)}) copy-start(s32[16]{0:T(128)} %param.21) | copy-start | bytes 196
  3.0 17.2 %copy-start.3 = (bf16[512,2,2,128]{3,2,1,0:T(2,128)(2,1)S(1)}, bf16[512,2,2,128]{3,2,1,0:T(2,128)(2,1)}, u32[]{:S(2)}) copy-start(bf16[512,2,2,128]{3,2,1,0:T(2,128)(2,1)} %param.16) | copy-start | bytes 1572868
  3.0 18.8 %copy-start.1 = (s32[16]{0:T(128)S(1)}, s32[16]{0:T(128)}, u32[]{:S(2)}) copy-start(s32[16]{0:T(128)} %param.18) | copy-start | bytes 196
  3.0 19.5 %copy-start.2 = (bf16[512,8,128]{2,1,0:T(8,128)(2,1)S(1)}, bf16[512,8,128]{2,1,0:T(8,128)(2,1)}, u32[]{:S(2)}) copy-start(bf16[512,8,128]{2,1,0:T(8,128)(2,1)} %param.15) | copy-start | bytes 3145732
  15.1 19.5 %all-to-all-start.1 = ((bf16[8,128,256]{2,1,0:T(8,128)(2,1)}), bf16[8,128,256]{2,1,0:T(8,128)(2,1)S(1)}, u32[]{:S(2)}, u32[]{:S(2)}) async-start(bf16[8,128,256]{2,1,0:T(8,128)(2,1)} %project.3), calls=%async_computation.1 | async-start | bytes 1048576 | tf_op jit(solution)/shard_map/all_to_all | solution.py:420
  34.6 12.5 %all-to-all-start = ((bf16[8,128,256]{2,1,0:T(8,128)(2,1)}), bf16[8,128,256]{2,1,0:T(8,128)(2,1)S(1)}, u32[]{:S(2)}, u32[]{:S(2)}) async-start(bf16[8,128,256]{2,1,0:T(8,128)(2,1)} %project.2), calls=%async_computation | async-start | bytes 1048576 | tf_op jit(solution)/shard_map/all_to_all | solution.py:420
